TPU v7x, 128 devices: a whole 4x4x4 slice. The times are simulated.
128 devices in a mesh: dp: 8 (over z_lo, x), vocab: 16 (over z_hi, y, core).
Axes of the slice: x: 4, y: 4, z: 4 (z_hi: 2, z_lo: 2; z = z_hi * 2 + z_lo), core: 2. Of those that a mesh axis runs over, the one named last changes fastest.
Arguments:
- hidden: bfloat16 [2, 8, 256, 4096], P(None, 'dp'), may hold values from -6 to 6
- weight: bfloat16 [32000, 4096], P('vocab'), may hold values from -0.09375 to 0.09375
- bias: float32 [32000], P('vocab'), may hold values from -1 to 0
- positions: int32 [2, 8, 32000], P(None, 'dp', 'vocab'), may hold values from 0 to 255
- lengths: int32 [2, 8], P(None, 'dp'), may hold values from 64 to 256
- pairs: int32 [8, 2], P('dp'), may hold values from 0 to 7
- margins: float32 [8], P('dp'), may hold values from -4 to 4
Outputs:
- grad_hidden: bfloat16 [2, 8, 256, 4096], P(None, 'dp', 'vocab')
- grad_weight: float32 [32000, 4096], P('vocab', 'dp')
Inputs may be any that keep to these rules, and one draw needn't show every extreme that they name: positions of tokens within a sequence, padded ones included. `pairs`: indices of passages in the whole batch; a pair's two may coincide.
All inputs are finite; a program needn't handle non-finite values.
Results may differ from a plain program's by a relative error of at most 0.02.
Values may be sent and summed in bfloat16 or wider, within the bound.
A program may use at most 128 MiB of HBM per device.

v0:
```python
import jax
import jax.numpy as jnp
from jax import lax
from jax.sharding import PartitionSpec as P

logit_divisor = 16.0
objective_factor = 256.0
regularizer_coefficient = 0.1


def local(hidden, weight, bias, positions, lengths, pairs, margins):
    per_dev = hidden.shape[1]
    seq_len = hidden.shape[2]
    groups = lax.axis_size("dp")
    total_batch = per_dev * groups
    logits = jnp.einsum("sbld,vd->lsbv", hidden, weight, preferred_element_type=jnp.float32) + bias
    token_pos = lax.broadcasted_iota(jnp.int32, (seq_len, 1, 1, 1), 0)
    picked = token_pos == positions[None]
    selected = jnp.sum(jnp.where(picked, logits, 0.0), axis=0)
    valid = positions < lengths[:, :, None]
    pooled = jnp.where(valid, jnp.log1p(jnp.maximum(selected, 0.0)), 0.0)
    request_vectors = pooled[0]
    gathered_passage_rows = lax.all_gather(pooled[1], "dp", axis=0, tiled=True)
    column_sums = lax.psum(jnp.sum(pooled, axis=1), "dp")
    means = column_sums / total_batch
    partway_result = jnp.dot(
        request_vectors, gathered_passage_rows.T, precision=lax.Precision.HIGHEST
    )
    relevance_logits = lax.psum(partway_result, "vocab") / logit_divisor
    columns = lax.broadcasted_iota(jnp.int32, (per_dev, total_batch), 1)
    sign = (columns == pairs[:, 0:1]).astype(jnp.float32) - (columns == pairs[:, 1:2]).astype(
        jnp.float32
    )
    delta = jnp.sum(relevance_logits * sign, axis=1)
    relevance_derivative = (objective_factor * 2.0 * (delta - margins) / total_batch)[
        :, None
    ] * sign
    request_derivative = (
        jnp.dot(relevance_derivative, gathered_passage_rows, precision=lax.Precision.HIGHEST)
        / logit_divisor
        + objective_factor * regularizer_coefficient * 2.0 * means[0] / total_batch
    )
    passage_expansion = (
        jnp.dot(relevance_derivative.T, request_vectors, precision=lax.Precision.HIGHEST)
        / logit_divisor
    )
    document_derivative = (
        lax.psum_scatter(
            passage_expansion.astype(jnp.bfloat16), "dp", scatter_dimension=0, tiled=True
        ).astype(jnp.float32)
        + objective_factor * regularizer_coefficient * 2.0 * means[1] / total_batch
    )
    drep = jnp.stack([request_derivative, document_derivative])
    dsel = jnp.where((selected > 0.0) & valid, drep / (1.0 + jnp.maximum(selected, 0.0)), 0.0)
    grad_rows = jnp.where(picked, dsel[None], 0.0).astype(jnp.bfloat16)
    summed = lax.psum_scatter(
        jnp.einsum("lsbv,vd->lsbd", grad_rows, weight, preferred_element_type=jnp.float32).astype(
            jnp.bfloat16
        ),
        "vocab",
        scatter_dimension=0,
        tiled=True,
    ).astype(jnp.float32)
    grad_hidden = jnp.transpose(summed, (1, 2, 0, 3)).astype(jnp.bfloat16)
    weight_term = jnp.einsum("lsbv,sbld->vd", grad_rows, hidden, preferred_element_type=jnp.float32)
    grad_weight = lax.psum_scatter(
        weight_term.astype(jnp.bfloat16), "dp", scatter_dimension=1, tiled=True
    ).astype(jnp.float32)
    return (grad_hidden, grad_weight)


def solution(mesh):
    in_specs = (
        P(None, "dp", None, None),
        P("vocab", None),
        P("vocab"),
        P(None, "dp", "vocab"),
        P(None, "dp"),
        P("dp", None),
        P("dp"),
    )
    out_specs = (P(None, "dp", "vocab", None), P("vocab", "dp"))
    return jax.shard_map(local, mesh=mesh, in_specs=in_specs, out_specs=out_specs, check_vma=False)
```

profile of v0, /device:TPU:2, one launch (start us, length us, event | category | flops | bytes accessed | tf_op | source)
XLA Modules:
  0.0 427.2 jit_solution(1156735496924421532)
XLA Ops:
  7.2 0.0 reduce-scatter.5.cloned.1.call-start
  7.2 0.7 copy.40
  7.9 0.0 copy-start
  8.0 0.0 copy-start.2
  8.0 0.0 copy-start.1
  8.0 0.0 copy-start.3
  8.0 14.0 %fusion.12 = f32[2,2000]{1,0:T(2,128)S(1)} fusion(bf16[2,1,256,4096]{3,2,1,0:T(8,128)(2,1)} %param.7, bf16[2000,4096]{1,0:T(8,128)(2,1)} %param.8, f32[2000]{0:T(1024)} %param.9, s32[2,2000]{1,0:T(2,128)S(1)} %bitcast.78), kind=kOutput, calls=%fused_computation.10 | convolution fusion | flops 8392699904 | bytes 20618304 | tf_op jit(solution)/shard_map/sbld,vd->lsbv/dot_general | solution.py:16
  22.1 0.0 copy-done
  22.1 0.0 copy-done.2
  22.1 0.1 bitcast_and_fusion
  22.3 28.7 %all-gather = f32[8,1,2000]{2,1,0:T(1,128)S(1)} all-gather(f32[1,1,2000]{2,1,0:T(1,128)S(1)} %get-tuple-element.10), channel_id=2, replica_groups=mesh['dp'=8,'vocab'=16] {'dp'}, dimensions={0}, use_global_device_ids=true | all-gather | bytes 72000 | tf_op jit(solution)/shard_map/all_gather | solution.py:23
  50.9 0.2 fusion.25
  51.1 33.5 %psum.14 = f32[1,8]{1,0:T(1,128)S(1)} all-reduce(f32[1,8]{1,0:T(1,128)S(1)} %fusion.25), channel_id=1, replica_groups=mesh['dp'=8,'vocab'=16] {'vocab'}, use_global_device_ids=true, to_apply=%region_1.2 | all-reduce | flops 8 | bytes 64 | tf_op jit(solution)/shard_map/psum | solution.py:29
  84.6 0.0 copy-done.1
  84.6 0.6 fusion.45
  85.9 2.0 multiply_reduce_fusion
  88.5 1.3 multiply_bitcast_fusion
  89.8 1.5 fusion.23
  91.3 0.1 multiply_convert_fusion
  91.4 29.9 %all-reduce = bf16[8,2000]{1,0:T(8,128)(2,1)S(1)} all-reduce(bf16[8,2000]{1,0:T(8,128)(2,1)S(1)} %multiply_convert_fusion), channel_id=3, replica_groups=mesh['dp'=8,'vocab'=16] {'dp'}, use_global_device_ids=true, to_apply=%region_4.5.clone | all-reduce | flops 16000 | bytes 64000
  121.3 32.8 %psum.15 = f32[2,2000]{1,0:T(2,128)S(1)} all-reduce(f32[2,2000]{1,0:T(2,128)S(1)} %bitcast.73), channel_id=1, replica_groups=mesh['dp'=8,'vocab'=16] {'dp'}, use_global_device_ids=true, to_apply=%region_3.4 | all-reduce | flops 4000 | bytes 32000 | tf_op jit(solution)/shard_map/psum | solution.py:24
  154.1 0.0 copy-done.3
  154.1 0.6 dynamic-slice
  154.7 0.7 slice_multiply_fusion.1
  155.5 14.1 %bitcast_convert_fusion = bf16[2000,4096]{1,0:T(8,128)(2,1)} fusion(bf16[2,1,256,4096]{3,2,1,0:T(8,128)(2,1)} %param.7, bf16[2,2000]{1,0:T(2,128)(2,1)S(1)} %bitcast.81, s32[2,2000]{1,0:T(2,128)S(1)} %bitcast.79), kind=kOutput, calls=%fused_computation | convolution fusion | flops 8398848000 | bytes 20602304 | tf_op jit(solution)/shard_map/lsbv,sbld->vd/dot_general | solution.py:65
  169.6 0.0 reduce-scatter.5.cloned.1.call-update
  169.6 0.2 reduce-scatter.3.cloned.1.call-start
  169.8 16.5 %fusion.7 = bf16[256,2,1,4096]{3,0,1,2:T(8,128)(2,1)} fusion(bf16[2000,4096]{1,0:T(8,128)(2,1)} %param.8, bf16[2,2000]{1,0:T(2,128)(2,1)S(1)} %bitcast.82, s32[2,2000]{1,0:T(2,128)S(1)} %bitcast.80), kind=kOutput, calls=%fused_computation.6 | convolution fusion | flops 8392753152 | bytes 20602304 | tf_op jit(solution)/shard_map/lsbv,vd->lsbd/dot_general | solution.py:57
  186.3 0.0 reduce-scatter.3.cloned.1.call-update
  186.3 147.4 %reduce-scatter.5.cloned.1.call-done = bf16[2000,512]{1,0:T(8,128)(2,1)} async-done(((bf16[2000,4096]{1,0:T(8,128)(2,1)}), bf16[2000,512]{1,0:T(8,128)(2,1)}) %reduce-scatter.5.cloned.1.call-update) | async-done | bytes 2048016 | tf_op jit(solution)/shard_map/reduce_scatter | solution.py:66
  333.7 4.1 convert_element_type.95
  337.9 82.5 %reduce-scatter.3.cloned.1.call-done = bf16[16,2,1,4096]{3,0,1,2:T(8,128)(2,1)} async-done(((bf16[256,2,1,4096]{3,0,1,2:T(8,128)(2,1)}), bf16[16,2,1,4096]{3,0,1,2:T(8,128)(2,1)}) %reduce-scatter.3.cloned.1.call-update) | async-done | bytes 262160 | tf_op jit(solution)/shard_map/reduce_scatter | solution.py:56
  (8 shorter events, 0.1 us)
Async XLA Ops:
  7.2 326.6 %reduce-scatter.5.cloned.1.call-start = ((), (), s32[]{:S(2)}) async-start(), calls=%async_computation.3 | async-start | bytes 18432000 | tf_op jit(solution)/shard_map/reduce_scatter | solution.py:66
  7.9 14.1 %copy-start = (s32[2,1,2000]{2,1,0:T(1,128)S(1)}, s32[2,1,2000]{2,1,0:T(1,128)}, u32[]{:S(2)}) copy-start(s32[2,1,2000]{2,1,0:T(1,128)} %param.10) | copy-start | bytes 48004
  8.0 14.1 %copy-start.2 = (s32[2,1]{0,1:T(1,128)S(1)}, s32[2,1]{0,1:T(1,128)}, u32[]{:S(2)}) copy-start(s32[2,1]{0,1:T(1,128)} %param.11) | copy-start | bytes 28
  8.0 76.7 %copy-start.1 = (s32[1,2]{1,0:T(1,128)S(1)}, s32[1,2]{1,0:T(1,128)}, u32[]{:S(2)}) copy-start(s32[1,2]{1,0:T(1,128)} %param.12) | copy-start | bytes 28
  8.0 146.1 %copy-start.3 = (u32[128]{0:T(128)S(1)}, u32[128]{0:T(128)}, u32[]{:S(2)}) copy-start(u32[128]{0:T(128)} %constant.34) | copy-start | bytes 1540
  169.6 250.8 %reduce-scatter.3.cloned.1.call-start = ((), (), s32[]{:S(2)}) async-start(), calls=%async_computation.2 | async-start | bytes 4456448 | tf_op jit(solution)/shard_map/reduce_scatter | solution.py:56
Sparse Core Ops, SparseCore 0:
  169.7 163.9 reduce-scatter.4
  338.9 81.4 reduce-scatter.2
where the time goes:
time: 428 us; the launch traced here: 427 us
  waiting for transfers between devices  230 us (54%)
  blocking collectives  125 us (29%)
  matrix products  46.3 us (11%)
  between operations  15.5 us (4%)
  other arithmetic  8.36 us (2%)
    reduce_scatter x1, waiting for transfers between devices, local(): lax.psum_scatter(weight_term.astype(jnp.bfloat16), 'dp', scatter_dimensio...  147 us
    reduce_scatter x1, waiting for transfers between devices, local(): lax.psum_scatter(jnp.einsum('lsbv,vd->lsbd', grad_rows, weight, preferred...  82.5 us
    psum x1, blocking collectives, local(): relevance_logits = lax.psum(partway_result, 'vocab') / logit_divisor  33.5 us
    psum x1, blocking collectives, local(): column_sums = lax.psum(jnp.sum(pooled, axis=1), 'dp')  32.8 us
    unnamed x1, blocking collectives  29.9 us
    all_gather x1, blocking collectives, local(): gathered_passage_rows = lax.all_gather(pooled[1], 'dp', axis=0, tiled=True)  28.7 us
    dot_general x1, matrix products, local(): jnp.einsum('lsbv,vd->lsbd', grad_rows, weight, preferred_element_type=jnp...  16.5 us
    dot_general x1, matrix products, local(): jnp.einsum('lsbv,sbld->vd', grad_rows, hidden, preferred_element_type=jnp...  14.1 us
  transfers between devices with their start and end apart: 2, of which 2 were waited for; matrix products, arithmetic and copies ran while one was open for 5% of the time, Pallas kernels for 0%

commit v1 on v0

v1 whole, which is shorter than its diff:
```python
import jax
import jax.numpy as jnp
from jax import lax
from jax.experimental import pallas as pl
from jax.experimental.pallas import tpu as pltpu
from jax.sharding import PartitionSpec as P

logit_divisor = 16.0
objective_factor = 256.0
regularizer_coefficient = 0.1

BF = jnp.bfloat16
F32 = jnp.float32
MESH = pl.DeviceIdType.MESH

V = 2000
VP = 2048
D = 4096
L = 256
NK = 8
NJ = 16
DB = 512
FC = 512
NF = VP // FC
HC = 512
NH = D // HC
HA = HC // 2
WC = 512
NW = VP // WC


def kernel(
    h_hbm,
    w_hbm,
    bias,
    pos_in,
    lens,
    pairs,
    margins,
    gh_out,
    gw_out,
    wv,
    hv,
    hx,
    g,
    gc,
    gwst,
    sibs,
    sibr,
    ownf,
    st,
    r1,
    r2,
    zst,
    r3,
    pm,
    sel,
    dl,
    qs,
    ps,
    ds,
    w_sem,
    h_sem,
    own_sem,
    gw_sem,
    pm_s,
    pm_r,
    hx_s,
    hx_r,
    fw_s,
    fw_r,
    sel_s,
    sel_r,
    dl_s,
    dl_r,
    sib_s,
    sib_r,
    y_s,
    y_r,
    z_s,
    z_r,
):
    k = lax.axis_index("dp")
    j = lax.axis_index("vocab")
    core = j % 2
    y = (j // 2) % 4
    zh = j // 8
    zl = k // 4
    x = k % 4

    def vid(zrel, yrel, crel):
        return ((zh + zrel) % 2) * 8 + ((y + yrel) % 4) * 2 + (core + crel) % 2

    def kid(dz, dx):
        return ((zl + dz) % 2) * 4 + (x + dx) % 4

    sibling = vid(0, 0, 1)
    up = vid(0, 1, 0)
    down = vid(0, 3, 0)
    across = vid(1, 0, 0)
    dp_steps = [(dz, dx) for dz in range(2) for dx in range(4) if (dz, dx) != (0, 0)]

    barrier = pltpu.get_barrier_semaphore()
    for dz, dx in dp_steps:
        pl.semaphore_signal(barrier, inc=1, device_id={"dp": kid(dz, dx)}, device_id_type=MESH)
    for i in range(1, NJ):
        pl.semaphore_signal(barrier, inc=1, device_id={"vocab": (j + i) % NJ}, device_id_type=MESH)

    h_copy = pltpu.make_async_copy(h_hbm, hv, h_sem)
    h_copy.start()
    w_copies = []
    for n in range(NF):
        rows = min(FC, V - n * FC)
        c = pltpu.make_async_copy(
            w_hbm.at[pl.ds(n * FC, rows), :], wv.at[pl.ds(n * FC, rows), :], w_sem.at[n]
        )
        c.start()
        w_copies.append(c)
    own_copy = pltpu.make_async_copy(
        h_hbm.at[:, pl.ds(pl.multiple_of(k * DB, DB), DB)], hx.at[k], own_sem
    )
    own_copy.start()
    wv[V:VP, :] = jnp.zeros((VP - V, D), BF)

    pad = jnp.zeros((1, VP - V), F32)
    for s in range(2):
        pm[k, s : s + 1, :] = jnp.concatenate([pos_in[s].astype(F32), pad], axis=1)
    pm[k, 2:3, 0:128] = jnp.full((1, 128), pairs[0, 0], jnp.int32).astype(F32)
    pm[k, 2:3, 128:256] = jnp.full((1, 128), pairs[0, 1], jnp.int32).astype(F32)
    pm[k, 2:3, 256:384] = jnp.full((1, 128), margins[0], F32)
    pm[k, 2:3, 384:VP] = jnp.zeros((1, VP - 384), F32)
    pm[k, 3:4, :] = jnp.zeros((1, VP), F32)

    pl.semaphore_wait(barrier, len(dp_steps) + NJ - 1)

    def to_dp(ref, ssem, rsem, i):
        dz, dx = dp_steps[i]
        return pltpu.make_async_remote_copy(
            src_ref=ref.at[k],
            dst_ref=ref.at[k],
            send_sem=ssem.at[i],
            recv_sem=rsem.at[i],
            device_id={"dp": kid(dz, dx)},
            device_id_type=MESH,
        )

    half = pl.ds(pl.multiple_of(core * L, L), L)

    def hx_copy(i):
        dz, dx = dp_steps[i]
        other = kid(dz, dx)
        return pltpu.make_async_remote_copy(
            src_ref=h_hbm.at[half, pl.ds(pl.multiple_of(other * DB, DB), DB)],
            dst_ref=hx.at[k, half, :],
            send_sem=hx_s.at[i],
            recv_sem=hx_r.at[i],
            device_id={"dp": other},
            device_id_type=MESH,
        )

    def fw_copy(i):
        dz, dx = dp_steps[i]
        src = kid(dz, 4 - dx)
        return pltpu.make_async_remote_copy(
            src_ref=hx.at[src, half, :],
            dst_ref=hx.at[src, half, :],
            send_sem=fw_s.at[i],
            recv_sem=fw_r.at[i],
            device_id={"vocab": sibling},
            device_id_type=MESH,
        )

    for i in range(7):
        to_dp(pm, pm_s, pm_r, i).start()
    for i in range(7):
        hx_copy(i).start()

    h_copy.wait()
    for n in range(NF):
        w_copies[n].wait()
        lg = lax.dot_general(
            hv[...],
            wv[n * FC : (n + 1) * FC, :],
            (((1,), (1,)), ((), ())),
            preferred_element_type=F32,
        )
        token = lax.broadcasted_iota(jnp.int32, (L, FC), 0).astype(F32)
        width = min(FC, V - n * FC)
        for s in range(2):
            spot = pm[k, s : s + 1, n * FC : (n + 1) * FC]
            picked = jnp.sum(
                jnp.where(token == spot, lg[s * L : (s + 1) * L], 0.0), axis=0, keepdims=True
            )
            b = bias[:, n * FC : n * FC + width]
            if width < FC:
                b = jnp.concatenate([b, jnp.zeros((1, FC - width), F32)], axis=1)
            valid = spot < lens[s, 0].astype(F32)
            sel[k, s : s + 1, n * FC : (n + 1) * FC] = jnp.where(
                valid, jnp.maximum(picked + b, 0.0), 0.0
            )

    for i in range(7):
        to_dp(sel, sel_s, sel_r, i).start()
    for i in range(7):
        to_dp(pm, pm_s, pm_r, i).wait()
    for i in range(7):
        to_dp(sel, sel_s, sel_r, i).wait()

    for i in range(NK):
        qs[i : i + 1, :] = sel[i, 0:1, :]
        ps[i : i + 1, :] = sel[i, 1:2, :]
    q = jnp.log1p(qs[...])
    p = jnp.log1p(ps[...])
    first = jnp.concatenate([pm[i, 2:3, 0:128] for i in range(NK)], axis=0)
    second = jnp.concatenate([pm[i, 2:3, 128:256] for i in range(NK)], axis=0)
    margin = jnp.concatenate([pm[i, 2:3, 256:384] for i in range(NK)], axis=0)

    def hit(a, b):
        return jnp.where(a == b, 1.0, 0.0)

    diff = jnp.zeros((NK, VP), F32)
    for i in range(NK):
        sign = hit(first, float(i)) - hit(second, float(i))
        diff += jnp.tile(sign, (1, VP // 128)) * p[i : i + 1, :]
    dl[j] = jnp.broadcast_to(jnp.sum(q * diff, axis=1, keepdims=True), (NK, 128))

    def dl_copy(i):
        return pltpu.make_async_remote_copy(
            src_ref=dl.at[j],
            dst_ref=dl.at[j],
            send_sem=dl_s.at[i],
            recv_sem=dl_r.at[i],
            device_id={"vocab": (j + i) % NJ},
            device_id_type=MESH,
        )

    for i in range(1, NJ):
        dl_copy(i).start()

    reg = objective_factor * regularizer_coefficient * 2.0 / NK / NK
    mean_q = reg * jnp.sum(q, axis=0, keepdims=True)
    mean_p = reg * jnp.sum(p, axis=0, keepdims=True)
    inv_q = jnp.where(qs[...] > 0.0, 1.0 / (1.0 + qs[...]), 0.0)
    inv_p = jnp.where(ps[...] > 0.0, 1.0 / (1.0 + ps[...]), 0.0)

    for i in range(1, NJ):
        dl_copy(i).wait()
    delta = dl[0]
    for i in range(1, NJ):
        delta += dl[i]
    delta = delta / logit_divisor
    weight_of = (objective_factor * 2.0 / NK / logit_divisor) * (delta - margin)
    ds[0] = (jnp.tile(weight_of, (1, VP // 128)) * diff + mean_q) * inv_q
    row = lax.broadcasted_iota(jnp.int32, (NK, 128), 0).astype(F32)
    dp = jnp.zeros((NK, VP), F32)
    for i in range(NK):
        sign = hit(first[i : i + 1, :], row) - hit(second[i : i + 1, :], row)
        dp += jnp.tile(sign * weight_of[i : i + 1, :], (1, VP // 128)) * q[i : i + 1, :]
    ds[1] = (dp + mean_p) * inv_p

    token16 = lax.broadcasted_iota(jnp.int32, (16, VP), 0).astype(F32)
    own_d = [ds[s, pl.ds(k, 1), :].astype(BF) for s in range(2)]
    own_p = [pm[k, s : s + 1, :].astype(BF) for s in range(2)]
    for crel in range(2):
        for yrel in range(4):
            for zrel in range(2):
                base = (vid(zrel, yrel, crel) * 16).astype(F32)
                token = (token16 + base).astype(BF)
                for s in range(2):
                    r = crel * 256 + yrel * 64 + zrel * 32 + s * 16
                    g[r : r + 16, :] = jnp.where(token == own_p[s], own_d[s], jnp.zeros((), BF))

    def sib_copy(c):
        return pltpu.make_async_remote_copy(
            src_ref=sibs.at[c],
            dst_ref=sibr.at[c],
            send_sem=sib_s.at[c],
            recv_sem=sib_r.at[c],
            device_id={"vocab": sibling},
            device_id_type=MESH,
        )

    def y_copy(c, which):
        src, dst, to = (
            (st.at[c, 128:192, 0:HA], r1.at[c, 0], up),
            (st.at[c, 128:192, HA:HC], r1.at[c, 1], down),
            (st.at[c, 64:128, HA:HC], r2.at[c, 0, :, HA:HC], up),
            (st.at[c, 192:256, 0:HA], r2.at[c, 1, :, 0:HA], down),
            (st.at[c, 64:128, 0:HA], r2.at[c, 0, :, 0:HA], up),
            (st.at[c, 192:256, HA:HC], r2.at[c, 1, :, HA:HC], down),
        )[which]
        return pltpu.make_async_remote_copy(
            src_ref=src,
            dst_ref=dst,
            send_sem=y_s.at[c, which],
            recv_sem=y_r.at[c, which],
            device_id={"vocab": to},
            device_id_type=MESH,
        )

    def z_copy(c):
        return pltpu.make_async_remote_copy(
            src_ref=zst.at[c],
            dst_ref=r3.at[c],
            send_sem=z_s.at[c],
            recv_sem=z_r.at[c],
            device_id={"vocab": across},
            device_id_type=MESH,
        )

    def pair_sum(c, rows, cols):
        return ownf[c, rows, cols] + sibr[c, rows, cols].astype(F32)

    lo, hi, both = slice(0, HA), slice(HA, HC), slice(0, HC)

    def stage1(c):
        sib_copy(c).wait_recv()
        st[c, 128:192, :] = pair_sum(c, slice(128, 192), both).astype(BF)
        y_copy(c, 0).start()
        y_copy(c, 1).start()
        st[c, 64:128, hi] = pair_sum(c, slice(64, 128), hi).astype(BF)
        y_copy(c, 2).start()
        st[c, 192:256, lo] = pair_sum(c, slice(192, 256), lo).astype(BF)
        y_copy(c, 3).start()

    def stage2(c):
        y_copy(c, 0).wait_recv()
        st[c, 64:128, lo] = (pair_sum(c, slice(64, 128), lo) + r1[c, 0].astype(F32)).astype(BF)
        y_copy(c, 4).start()
        y_copy(c, 1).wait_recv()
        st[c, 192:256, hi] = (pair_sum(c, slice(192, 256), hi) + r1[c, 1].astype(F32)).astype(BF)
        y_copy(c, 5).start()

    def stage3(c):
        for which in (2, 3, 4, 5):
            y_copy(c, which).wait_recv()
        far = slice(32, 64)
        zst[c] = (
            pair_sum(c, far, both) + r2[c, 0, far].astype(F32) + r2[c, 1, far].astype(F32)
        ).astype(BF)
        z_copy(c).start()
        near = slice(0, 32)
        ownf[c, near, :] = (
            pair_sum(c, near, both) + r2[c, 0, near].astype(F32) + r2[c, 1, near].astype(F32)
        )

    def stage4(c):
        z_copy(c).wait_recv()
        total = (ownf[c, 0:32, :] + r3[c].astype(F32)).astype(BF)
        cols = pl.ds(pl.multiple_of(c * HC, HC), HC)
        gh_out[0, :, cols] = total[0:16]
        gh_out[1, :, cols] = total[16:32]

    def when(cond):
        return pl.when(cond)

    def gh_step(c, carry):
        cols = pl.ds(pl.multiple_of(c * HC, HC), HC)
        part = jnp.dot(g[...], wv[:, cols], preferred_element_type=F32)
        sibs[c] = part[256:512].astype(BF)
        sib_copy(c).start()
        ownf[c] = part[0:256]

        @when(c >= 1)
        def _():
            stage1(c - 1)

        @when(c >= 4)
        def _():
            stage2(c - 4)

        return carry

    lax.fori_loop(0, NH, gh_step, 0)
    stage1(NH - 1)

    for i in range(7):
        hx_copy(i).wait_recv()
        fw_copy(i).start()
    own_copy.wait()
    for i in range(7):
        fw_copy(i).wait_recv()

    token256 = lax.broadcasted_iota(jnp.int32, (L, WC), 0).astype(F32).astype(BF)

    def gw_copy(n, slot, rows):
        return pltpu.make_async_copy(
            gwst.at[slot, 0:rows, :],
            gw_out.at[pl.ds(pl.multiple_of(n * WC, WC), rows), :],
            gw_sem.at[slot],
        )

    tail = V - (NW - 1) * WC

    def gw_step(n, carry):
        slot = n % 2
        cols = pl.ds(pl.multiple_of(n * WC, WC), WC)
        for i in range(NK):
            for s in range(2):
                spot = pm[i, s : s + 1, cols].astype(BF)
                val = ds[s, i : i + 1, cols].astype(BF)
                r = (i * 2 + s) * L
                gc[r : r + L, :] = jnp.where(token256 == spot, val, jnp.zeros((), BF))
        out = lax.dot_general(
            gc[...],
            hx[...].reshape(NK * 2 * L, DB),
            (((0,), (0,)), ((), ())),
            preferred_element_type=F32,
        )

        @when(n >= 2)
        def _():
            gw_copy(n - 2, slot, WC).wait()

        gwst[slot] = out

        @when(n < NW - 1)
        def _():
            gw_copy(n, slot, WC).start()

        @when(n == NW - 1)
        def _():
            gw_copy(n, slot, tail).start()

        @when(n < 2)
        def _():
            stage2(4 + 2 * n)
            stage2(5 + 2 * n)

        stage3(2 * n)
        stage3(2 * n + 1)

        @when(n >= 1)
        def _():
            stage4(2 * n - 2)
            stage4(2 * n - 1)

        return carry

    lax.fori_loop(0, NW, gw_step, 0)
    stage4(NH - 2)
    stage4(NH - 1)

    gw_copy(NW - 2, (NW - 2) % 2, WC).wait()
    gw_copy(NW - 1, (NW - 1) % 2, tail).wait()
    for i in range(7):
        hx_copy(i).wait_send()
        fw_copy(i).wait_send()

    def drain(c, carry):
        sib_copy(c).wait_send()
        for which in range(6):
            y_copy(c, which).wait_send()
        z_copy(c).wait_send()
        return carry

    lax.fori_loop(0, NH, drain, 0)


def local(hidden, weight, bias, positions, lengths, pairs, margins):
    vmem = pl.BlockSpec(memory_space=pltpu.VMEM)
    smem = pl.BlockSpec(memory_space=pltpu.SMEM)
    hbm = pl.BlockSpec(memory_space=pl.ANY)
    dma = pltpu.SemaphoreType.DMA
    scratch = [
        pltpu.VMEM((VP, D), BF),
        pltpu.VMEM((2 * L, D), BF),
        pltpu.VMEM((NK, 2 * L, DB), BF),
        pltpu.VMEM((2 * L, VP), BF),
        pltpu.VMEM((NK * 2 * L, WC), BF),
        pltpu.VMEM((2, WC, DB), F32),
        pltpu.VMEM((NH, 256, HC), BF),
        pltpu.VMEM((NH, 256, HC), BF),
        pltpu.VMEM((NH, 256, HC), F32),
        pltpu.VMEM((NH, 256, HC), BF),
        pltpu.VMEM((NH, 2, 64, HA), BF),
        pltpu.VMEM((NH, 2, 64, HC), BF),
        pltpu.VMEM((NH, 32, HC), BF),
        pltpu.VMEM((NH, 32, HC), BF),
        pltpu.VMEM((NK, 4, VP), F32),
        pltpu.VMEM((NK, 2, VP), F32),
        pltpu.VMEM((NJ, NK, 128), F32),
        pltpu.VMEM((NK, VP), F32),
        pltpu.VMEM((NK, VP), F32),
        pltpu.VMEM((2, NK, VP), F32),
        dma((NF,)),
        dma,
        dma,
        dma((2,)),
        dma((7,)),
        dma((7,)),
        dma((7,)),
        dma((7,)),
        dma((7,)),
        dma((7,)),
        dma((7,)),
        dma((7,)),
        dma((NJ,)),
        dma((NJ,)),
        dma((NH,)),
        dma((NH,)),
        dma((NH, 6)),
        dma((NH, 6)),
        dma((NH,)),
        dma((NH,)),
    ]
    gh, gw = pl.pallas_call(
        kernel,
        out_shape=(
            jax.ShapeDtypeStruct((2, 16, D), BF),
            jax.ShapeDtypeStruct((V, DB), F32),
        ),
        in_specs=[hbm, hbm, vmem, vmem, smem, smem, smem],
        out_specs=(vmem, hbm),
        scratch_shapes=scratch,
        compiler_params=pltpu.CompilerParams(
            collective_id=0, has_side_effects=True, vmem_limit_bytes=62 * 2**20
        ),
        cost_estimate=pl.CostEstimate(
            flops=6 * 512 * V * D, bytes_accessed=24 * 2**20, transcendentals=0
        ),
        name="splade_backward",
    )(
        hidden.reshape(2 * L, D),
        weight,
        bias.reshape(1, V),
        positions,
        lengths,
        pairs,
        margins,
    )
    return gh.reshape(2, 1, 16, D), gw


def solution(mesh):
    in_specs = (
        P(None, "dp", None, None),
        P("vocab", None),
        P("vocab"),
        P(None, "dp", "vocab"),
        P(None, "dp"),
        P("dp", None),
        P("dp"),
    )
    out_specs = (P(None, "dp", "vocab", None), P("vocab", "dp"))
    return jax.shard_map(local, mesh=mesh, in_specs=in_specs, out_specs=out_specs, check_vma=False)
```

time: 428 us -> 94.3 us (0.22)
  waiting for transfers between devices: 230 us -> 0 us
  blocking collectives: 125 us -> 0 us
  Pallas kernels: 0 us -> 85.2 us
  matrix products: 46.3 us -> 0 us
  between operations: 15.5 us -> 1.29 us
  other arithmetic: 8.36 us -> 0 us
  local copies, waits for them, and re-layouts: 1.94 us -> 7.53 us
    reduce_scatter x2 -> x0, waiting for transfers between devices: 230 us -> none  [the longest x1 147 us: local(): lax.psum_scatter(weight_term.astype(jnp.bfloat16), 'dp', scatter_dimensio...]
    pallas_call x0 -> x1, Pallas kernels: none -> 85.2 us  [local(): pl.pallas_call(kernel, out_shape=(jax.ShapeDtypeStruct((2, 16, D), BF), j...]
    psum x2 -> x0, blocking collectives: 66.3 us -> none  [the longest x1 33.5 us: local(): relevance_logits = lax.psum(partway_result, 'vocab') / logit_divisor]
    dot_general x5 -> x0, matrix products: 46.3 us -> none  [the longest x1 16.5 us: local(): jnp.einsum('lsbv,vd->lsbd', grad_rows, weight, preferred_element_type=jnp...]
    unnamed x1 -> x0, blocking collectives: 29.9 us -> none
    all_gather x1 -> x0, blocking collectives: 28.7 us -> none  [local(): gathered_passage_rows = lax.all_gather(pooled[1], 'dp', axis=0, tiled=True)]
    unnamed x12 -> x3, local copies, waits for them, and re-layouts: 1.36 us -> 7.53 us
  transfers between devices with their start and end apart: 2 -> 0, of which waited for: 2 -> 0; matrix products, arithmetic and copies ran while one was open for 5% -> 0% of each run, Pallas kernels for 0% -> 0%
where the time goes in v1:
time: 94.3 us; the launch traced here: 94 us
  Pallas kernels  85.2 us (90%)
  local copies, waits for them, and re-layouts  7.53 us (8%)
  between operations  1.29 us (1%)
    pallas_call x1, Pallas kernels, local(): pl.pallas_call(kernel, out_shape=(jax.ShapeDtypeStruct((2, 16, D), BF), j...  85.2 us
    unnamed x3, local copies, waits for them, and re-layouts  7.53 us

profile of v1, /device:TPU:2, one launch (start us, length us, event | category | flops | bytes accessed | tf_op | source)
XLA Modules:
  0.0 94.0 jit_solution(17404374122283114986)
XLA Ops:
  1.3 1.3 %copy.9.lens = s32[2,1]{1,0:T(2,128)} copy(s32[2,1]{0,1:T(1,128)} %param.11) | data formatting | bytes 16 | tf_op args[4]
  2.6 85.2 %splade_backward.1 = (bf16[2,16,4096]{2,1,0:T(8,128)(2,1)}, f32[2000,512]{1,0:T(8,128)}) custom-call(bf16[512,4096]{1,0:T(8,128)(2,1)} %bitcast.6, bf16[2000,4096]{1,0:T(8,128)(2,1)} %w_hbm.1, f32[1,2000]{1,0:T(1,128)} %bitcast.7, s32[2,1,2000]{2,1,0:T(1,128)} %pos_in.1, s32[2,1]{1,0:T(2,128)} %copy.9.lens, s32[1,2]{1,0:T(1,128)} %pairs.1, f32[1]{0:T(128)S(6)} %copy.13.margins), custom_call_target="tpu_custom_call" | custom-call | flops 25165824000 | bytes 25165824 | tf_op jit(solution)/shard_map/splade_backward/pallas_call | solution.py:507
  87.8 1.7 %copy.14 = bf16[2,1,16,4096]{3,2,1,0:T(8,128)(2,1)} copy(bf16[2,1,16,4096]{3,2,1,0:T(8,128)(2,1)} %bitcast.5) | data formatting | bytes 524288
  89.5 4.6 %copy.15 = f32[2000,512]{1,0:T(8,128)} copy(f32[2000,512]{1,0:T(8,128)} %get-tuple-element.11) | data formatting | bytes 8192000

commit v2 on v1

--- a/solution.py
+++ b/solution.py
@@ -20,13 +20,14 @@
 NK = 8
 NJ = 16
 DB = 512
-FC = 512
-NF = VP // FC
+FWD = ((0, 256), (256, 256), (512, 512), (1024, 512), (1536, 512))
+NF = len(FWD)
 HC = 512
 NH = D // HC
 HA = HC // 2
 WC = 512
 NW = VP // WC
+CP = 5
 
 
 def kernel(
@@ -103,35 +104,42 @@
     barrier = pltpu.get_barrier_semaphore()
     for dz, dx in dp_steps:
         pl.semaphore_signal(barrier, inc=1, device_id={"dp": kid(dz, dx)}, device_id_type=MESH)
+    for dx in range(4):
+        pl.semaphore_signal(
+            barrier,
+            inc=1,
+            device_id={"dp": kid(1, dx), "vocab": across},
+            device_id_type=MESH,
+        )
     for i in range(1, NJ):
         pl.semaphore_signal(barrier, inc=1, device_id={"vocab": (j + i) % NJ}, device_id_type=MESH)
 
     h_copy = pltpu.make_async_copy(h_hbm, hv, h_sem)
     h_copy.start()
     w_copies = []
-    for n in range(NF):
-        rows = min(FC, V - n * FC)
+    for n, (at, size) in enumerate(FWD):
+        rows = min(size, V - at)
         c = pltpu.make_async_copy(
-            w_hbm.at[pl.ds(n * FC, rows), :], wv.at[pl.ds(n * FC, rows), :], w_sem.at[n]
-        )
-        c.start()
+            w_hbm.at[pl.ds(at, rows), :], wv.at[pl.ds(at, rows), :], w_sem.at[n]
+        )
         w_copies.append(c)
+    w_copies[0].start()
+    w_copies[1].start()
     own_copy = pltpu.make_async_copy(
-        h_hbm.at[:, pl.ds(pl.multiple_of(k * DB, DB), DB)], hx.at[k], own_sem
+        hv.at[core, :, :, :, pl.ds(pl.multiple_of(k * DB, DB), DB)],
+        hx.at[k, core],
+        own_sem,
     )
-    own_copy.start()
     wv[V:VP, :] = jnp.zeros((VP - V, D), BF)
 
     pad = jnp.zeros((1, VP - V), F32)
     for s in range(2):
         pm[k, s : s + 1, :] = jnp.concatenate([pos_in[s].astype(F32), pad], axis=1)
-    pm[k, 2:3, 0:128] = jnp.full((1, 128), pairs[0, 0], jnp.int32).astype(F32)
-    pm[k, 2:3, 128:256] = jnp.full((1, 128), pairs[0, 1], jnp.int32).astype(F32)
+    pm[k, 2:3, 0:128] = jnp.full((1, 128), pairs[0], jnp.int32).astype(F32)
+    pm[k, 2:3, 128:256] = jnp.full((1, 128), pairs[1], jnp.int32).astype(F32)
     pm[k, 2:3, 256:384] = jnp.full((1, 128), margins[0], F32)
     pm[k, 2:3, 384:VP] = jnp.zeros((1, VP - 384), F32)
     pm[k, 3:4, :] = jnp.zeros((1, VP), F32)
-
-    pl.semaphore_wait(barrier, len(dp_steps) + NJ - 1)
 
     def to_dp(ref, ssem, rsem, i):
         dz, dx = dp_steps[i]
@@ -144,60 +152,85 @@
             device_id_type=MESH,
         )
 
-    half = pl.ds(pl.multiple_of(core * L, L), L)
-
-    def hx_copy(i):
+    near = [(i, None, None) for i in range(7) if dp_steps[i][0] == 0]
+    far = [
+        [(i, part, sub) for i in range(7) if dp_steps[i][0] == 1 for part in range(2)]
+        for sub in range(2)
+    ]
+
+    def hx_copy(i, part, sub):
         dz, dx = dp_steps[i]
         other = kid(dz, dx)
+        cols = pl.ds(pl.multiple_of(other * DB, DB), DB)
+        if part is None:
+            src, dst, sems = hv.at[core, :, :, :, cols], hx.at[k, core], (i, 0, 0)
+            to = {"dp": other}
+        else:
+            src, dst = hv.at[core, part, sub, :, cols], hx.at[k, core, part, sub]
+            sems, to = (i, part, sub), {"dp": other, "vocab": vid(part, 0, 0)}
         return pltpu.make_async_remote_copy(
-            src_ref=h_hbm.at[half, pl.ds(pl.multiple_of(other * DB, DB), DB)],
-            dst_ref=hx.at[k, half, :],
-            send_sem=hx_s.at[i],
-            recv_sem=hx_r.at[i],
-            device_id={"dp": other},
-            device_id_type=MESH,
-        )
-
-    def fw_copy(i):
-        dz, dx = dp_steps[i]
-        src = kid(dz, 4 - dx)
+            src_ref=src,
+            dst_ref=dst,
+            send_sem=hx_s.at[sems],
+            recv_sem=hx_r.at[sems],
+            device_id=to,
+            device_id_type=MESH,
+        )
+
+    def fw_copy(which):
+        if which == 0:
+            ref = hx.at[pl.ds(zl * 4, 4), core]
+        else:
+            ref = hx.at[pl.ds((1 - zl) * 4, 4), core, :, which - 1]
         return pltpu.make_async_remote_copy(
-            src_ref=hx.at[src, half, :],
-            dst_ref=hx.at[src, half, :],
-            send_sem=fw_s.at[i],
-            recv_sem=fw_r.at[i],
+            src_ref=ref,
+            dst_ref=ref,
+            send_sem=fw_s.at[which],
+            recv_sem=fw_r.at[which],
             device_id={"vocab": sibling},
             device_id_type=MESH,
         )
 
-    for i in range(7):
-        to_dp(pm, pm_s, pm_r, i).start()
-    for i in range(7):
-        hx_copy(i).start()
+    def pass_on(which):
+        if which == 0:
+            own_copy.wait()
+            batch = near
+        else:
+            batch = far[which - 1]
+        for item in batch:
+            hx_copy(*item).wait_recv()
+        fw_copy(which).start()
 
     h_copy.wait()
-    for n in range(NF):
+    for n, (at, size) in enumerate(FWD):
         w_copies[n].wait()
+        if n + 2 < NF:
+            w_copies[n + 2].start()
         lg = lax.dot_general(
-            hv[...],
-            wv[n * FC : (n + 1) * FC, :],
+            hv[...].reshape(2 * L, D),
+            wv[at : at + size, :],
             (((1,), (1,)), ((), ())),
             preferred_element_type=F32,
         )
-        token = lax.broadcasted_iota(jnp.int32, (L, FC), 0).astype(F32)
-        width = min(FC, V - n * FC)
+        token = lax.broadcasted_iota(jnp.int32, (L, size), 0).astype(F32)
+        width = min(size, V - at)
         for s in range(2):
-            spot = pm[k, s : s + 1, n * FC : (n + 1) * FC]
+            spot = pm[k, s : s + 1, at : at + size]
             picked = jnp.sum(
                 jnp.where(token == spot, lg[s * L : (s + 1) * L], 0.0), axis=0, keepdims=True
             )
-            b = bias[:, n * FC : n * FC + width]
-            if width < FC:
-                b = jnp.concatenate([b, jnp.zeros((1, FC - width), F32)], axis=1)
-            valid = spot < lens[s, 0].astype(F32)
-            sel[k, s : s + 1, n * FC : (n + 1) * FC] = jnp.where(
-                valid, jnp.maximum(picked + b, 0.0), 0.0
-            )
+            b = bias[:, at : at + width]
+            if width < size:
+                b = jnp.concatenate([b, jnp.zeros((1, size - width), F32)], axis=1)
+            valid = spot < lens[s].astype(F32)
+            sel[k, s : s + 1, at : at + size] = jnp.where(valid, jnp.maximum(picked + b, 0.0), 0.0)
+        if n == 1:
+            pl.semaphore_wait(barrier, len(dp_steps) + 4 + NJ - 1)
+            for i in range(7):
+                to_dp(pm, pm_s, pm_r, i).start()
+            for item in far[0]:
+                hx_copy(*item).start()
+            own_copy.start()
 
     for i in range(7):
         to_dp(sel, sel_s, sel_r, i).start()
@@ -205,6 +238,8 @@
         to_dp(pm, pm_s, pm_r, i).wait()
     for i in range(7):
         to_dp(sel, sel_s, sel_r, i).wait()
+    for item in near:
+        hx_copy(*item).start()
 
     for i in range(NK):
         qs[i : i + 1, :] = sel[i, 0:1, :]
@@ -334,14 +369,14 @@
     def stage3(c):
         for which in (2, 3, 4, 5):
             y_copy(c, which).wait_recv()
-        far = slice(32, 64)
+        away = slice(32, 64)
         zst[c] = (
-            pair_sum(c, far, both) + r2[c, 0, far].astype(F32) + r2[c, 1, far].astype(F32)
+            pair_sum(c, away, both) + r2[c, 0, away].astype(F32) + r2[c, 1, away].astype(F32)
         ).astype(BF)
         z_copy(c).start()
-        near = slice(0, 32)
-        ownf[c, near, :] = (
-            pair_sum(c, near, both) + r2[c, 0, near].astype(F32) + r2[c, 1, near].astype(F32)
+        here = slice(0, 32)
+        ownf[c, here, :] = (
+            pair_sum(c, here, both) + r2[c, 0, here].astype(F32) + r2[c, 1, here].astype(F32)
         )
 
     def stage4(c):
@@ -369,17 +404,27 @@
         def _():
             stage2(c - 4)
 
+        @when(c == 0)
+        def _():
+            for item in far[1]:
+                hx_copy(*item).start()
+
+        @when(c == 2)
+        def _():
+            pass_on(1)
+
+        @when(c == 7)
+        def _():
+            pass_on(0)
+
         return carry
 
     lax.fori_loop(0, NH, gh_step, 0)
     stage1(NH - 1)
 
-    for i in range(7):
-        hx_copy(i).wait_recv()
-        fw_copy(i).start()
-    own_copy.wait()
-    for i in range(7):
-        fw_copy(i).wait_recv()
+    pass_on(2)
+    for which in range(3):
+        fw_copy(which).wait_recv()
 
     token256 = lax.broadcasted_iota(jnp.int32, (L, WC), 0).astype(F32).astype(BF)
 
@@ -443,9 +488,10 @@
 
     gw_copy(NW - 2, (NW - 2) % 2, WC).wait()
     gw_copy(NW - 1, (NW - 1) % 2, tail).wait()
-    for i in range(7):
-        hx_copy(i).wait_send()
-        fw_copy(i).wait_send()
+    for item in near + far[0] + far[1]:
+        hx_copy(*item).wait_send()
+    for which in range(3):
+        fw_copy(which).wait_send()
 
     def drain(c, carry):
         sib_copy(c).wait_send()
@@ -455,6 +501,22 @@
         return carry
 
     lax.fori_loop(0, NH, drain, 0)
+
+
+def finish(gh_in, gw_in, gh_out, gw_out, gh_v, gw_v, in_sem, out_sem):
+    ins = [pltpu.make_async_copy(gh_in, gh_v, in_sem.at[CP])]
+    outs = [pltpu.make_async_copy(gh_v, gh_out, out_sem.at[CP])]
+    for i in range(CP):
+        rows = pl.ds(i * (V // CP), V // CP)
+        ins.append(pltpu.make_async_copy(gw_in.at[rows, :], gw_v.at[rows, :], in_sem.at[i]))
+        outs.append(pltpu.make_async_copy(gw_v.at[rows, :], gw_out.at[rows, :], out_sem.at[i]))
+    for c in ins:
+        c.start()
+    for a, b in zip(ins, outs):
+        a.wait()
+        b.start()
+    for c in outs:
+        c.wait()
 
 
 def local(hidden, weight, bias, positions, lengths, pairs, margins):
@@ -464,8 +526,8 @@
     dma = pltpu.SemaphoreType.DMA
     scratch = [
         pltpu.VMEM((VP, D), BF),
-        pltpu.VMEM((2 * L, D), BF),
-        pltpu.VMEM((NK, 2 * L, DB), BF),
+        pltpu.VMEM((2, 2, 2, L // 4, D), BF),
+        pltpu.VMEM((NK, 2, 2, 2, L // 4, DB), BF),
         pltpu.VMEM((2 * L, VP), BF),
         pltpu.VMEM((NK * 2 * L, WC), BF),
         pltpu.VMEM((2, WC, DB), F32),
@@ -489,10 +551,10 @@
         dma((2,)),
         dma((7,)),
         dma((7,)),
-        dma((7,)),
-        dma((7,)),
-        dma((7,)),
-        dma((7,)),
+        dma((7, 2, 2)),
+        dma((7, 2, 2)),
+        dma((3,)),
+        dma((3,)),
         dma((7,)),
         dma((7,)),
         dma((NJ,)),
@@ -521,14 +583,31 @@
         ),
         name="splade_backward",
     )(
-        hidden.reshape(2 * L, D),
+        hidden.reshape(2, 2, 2, L // 4, D),
         weight,
         bias.reshape(1, V),
         positions,
-        lengths,
-        pairs,
+        lengths.reshape(2),
+        pairs.reshape(2),
         margins,
     )
+    gh, gw = pl.pallas_call(
+        finish,
+        out_shape=(
+            jax.ShapeDtypeStruct((2, 16, D), BF),
+            jax.ShapeDtypeStruct((V, DB), F32),
+        ),
+        in_specs=[hbm, hbm],
+        out_specs=(hbm, hbm),
+        scratch_shapes=[
+            pltpu.VMEM((2, 16, D), BF),
+            pltpu.VMEM((V, DB), F32),
+            dma((CP + 1,)),
+            dma((CP + 1,)),
+        ],
+        compiler_params=pltpu.CompilerParams(vmem_limit_bytes=62 * 2**20),
+        name="finish",
+    )(gh, gw)
     return gh.reshape(2, 1, 16, D), gw
 
 

time: 94.3 us -> 71.5 us (0.76); the launches traced: 94 us -> 70.2 us
  Pallas kernels: 85.2 us -> 68.9 us
  local copies, waits for them, and re-layouts: 7.53 us -> 0 us
    pallas_call x1, Pallas kernels: 85.2 us -> 65.2 us  [local(): pl.pallas_call(kernel, out_shape=(jax.ShapeDtypeStruct((2, 16, D), BF), j...]
    unnamed x3 -> x0, local copies, waits for them, and re-layouts: 7.53 us -> none
    pallas_call x0 -> x1, Pallas kernels: none -> 3.71 us  [local(): pl.pallas_call(finish, out_shape=(jax.ShapeDtypeStruct((2, 16, D), BF), j...]
where the time goes in v2:
time: 71.5 us; the launch traced here: 70.2 us
  Pallas kernels  68.9 us (96%)
  between operations  1.29 us (2%)
    pallas_call x1, Pallas kernels, local(): pl.pallas_call(kernel, out_shape=(jax.ShapeDtypeStruct((2, 16, D), BF), j...  65.2 us
    pallas_call x1, Pallas kernels, local(): pl.pallas_call(finish, out_shape=(jax.ShapeDtypeStruct((2, 16, D), BF), j...  3.71 us

profile of v2, /device:TPU:2, one launch (start us, length us, event | category | flops | bytes accessed | tf_op | source)
XLA Modules:
  0.0 70.2 jit_solution(9215438470755059679)
XLA Ops:
  1.3 65.2 %splade_backward.1 = (bf16[2,16,4096]{2,1,0:T(8,128)(2,1)}, f32[2000,512]{1,0:T(8,128)}) custom-call(bf16[2,2,2,64,4096]{4,3,2,1,0:T(8,128)(2,1)} %bitcast.7, bf16[2000,4096]{1,0:T(8,128)(2,1)} %w_hbm.1, f32[1,2000]{1,0:T(1,128)} %bitcast.9, s32[2,1,2000]{2,1,0:T(1,128)} %pos_in.1, s32[2]{0:T(128)} %bitcast.10, s32[2]{0:T(128)} %bitcast.11, f32[1]{0:T(128)S(6)} %copy.10.margins), custom_call_target="tpu_custom_call" | custom-call | flops 25165824000 | bytes 25165824 | tf_op jit(solution)/shard_map/splade_backward/pallas_call | solution.py:569
  66.5 3.7 %finish.1 = (bf16[2,16,4096]{2,1,0:T(8,128)(2,1)}, f32[2000,512]{1,0:T(8,128)}) custom-call(bf16[2,16,4096]{2,1,0:T(8,128)(2,1)} %get-tuple-element.6.gh_in, f32[2000,512]{1,0:T(8,128)} %get-tuple-element.7.gw_in), custom_call_target="tpu_custom_call" | custom-call | tf_op jit(solution)/shard_map/finish/pallas_call | solution.py:594

commit v3 on v2

--- a/solution.py
+++ b/solution.py
@@ -20,14 +20,31 @@
 NK = 8
 NJ = 16
 DB = 512
-FWD = ((0, 256), (256, 256), (512, 512), (1024, 512), (1536, 512))
+FWD = ((0, 256), (256, 256), (512, 512), (1024, 1024))
 NF = len(FWD)
 HC = 512
 NH = D // HC
-HA = HC // 2
 WC = 512
 NW = VP // WC
-CP = 5
+ZFIRST = (0, 3, 7)
+TURN = (0, 1, 0, 1, 1, 0, 1, 0)
+FORTH, BACK = (64, 192), (192, 64)
+PLAN = {
+    2: ((0, 1),),
+    3: ((1, 1),),
+    4: ((2, 1),),
+    5: ((3, 1),),
+    6: ((1, 2), (4, 1), (5, 1)),
+    7: ((0, 2), (2, 2)),
+    8: ((1, 3), (6, 1), (7, 1)),
+    9: ((3, 2), (4, 2), (5, 2)),
+    10: ((0, 3),),
+    11: ((1, 4), (2, 3), (6, 2)),
+    12: ((3, 3), (7, 2)),
+    13: ((0, 4), (4, 3), (5, 3)),
+    14: ((2, 4), (3, 4), (6, 3), (7, 3)),
+    15: ((4, 4), (5, 4), (7, 4), (6, 4)),
+}
 
 
 def kernel(
@@ -45,7 +62,6 @@
     hx,
     g,
     gc,
-    gwst,
     sibs,
     sibr,
     ownf,
@@ -63,7 +79,6 @@
     w_sem,
     h_sem,
     own_sem,
-    gw_sem,
     pm_s,
     pm_r,
     hx_s,
@@ -202,6 +217,12 @@
         fw_copy(which).start()
 
     h_copy.wait()
+    pl.semaphore_wait(barrier, len(dp_steps) + 4 + NJ - 1)
+    for i in range(7):
+        to_dp(pm, pm_s, pm_r, i).start()
+    for item in far[0]:
+        hx_copy(*item).start()
+    own_copy.start()
     for n, (at, size) in enumerate(FWD):
         w_copies[n].wait()
         if n + 2 < NF:
@@ -224,13 +245,6 @@
                 b = jnp.concatenate([b, jnp.zeros((1, size - width), F32)], axis=1)
             valid = spot < lens[s].astype(F32)
             sel[k, s : s + 1, at : at + size] = jnp.where(valid, jnp.maximum(picked + b, 0.0), 0.0)
-        if n == 1:
-            pl.semaphore_wait(barrier, len(dp_steps) + 4 + NJ - 1)
-            for i in range(7):
-                to_dp(pm, pm_s, pm_r, i).start()
-            for item in far[0]:
-                hx_copy(*item).start()
-            own_copy.start()
 
     for i in range(7):
         to_dp(sel, sel_s, sel_r, i).start()
@@ -305,6 +319,9 @@
                     r = crel * 256 + yrel * 64 + zrel * 32 + s * 16
                     g[r : r + 16, :] = jnp.where(token == own_p[s], own_d[s], jnp.zeros((), BF))
 
+    def height(c):
+        return 32 if c in ZFIRST else 64
+
     def sib_copy(c):
         return pltpu.make_async_remote_copy(
             src_ref=sibs.at[c],
@@ -316,207 +333,159 @@
         )
 
     def y_copy(c, which):
-        src, dst, to = (
-            (st.at[c, 128:192, 0:HA], r1.at[c, 0], up),
-            (st.at[c, 128:192, HA:HC], r1.at[c, 1], down),
-            (st.at[c, 64:128, HA:HC], r2.at[c, 0, :, HA:HC], up),
-            (st.at[c, 192:256, 0:HA], r2.at[c, 1, :, 0:HA], down),
-            (st.at[c, 64:128, 0:HA], r2.at[c, 0, :, 0:HA], up),
-            (st.at[c, 192:256, HA:HC], r2.at[c, 1, :, HA:HC], down),
-        )[which]
+        n = height(c)
+        side = TURN[c]
+        src = st.at[c, pl.ds((128, BACK[side], FORTH[side])[which], n)]
+        if which == 0:
+            dst = r1.at[c, 0:n]
+        else:
+            dst = r2.at[c, which - 1, 0:n]
         return pltpu.make_async_remote_copy(
             src_ref=src,
             dst_ref=dst,
             send_sem=y_s.at[c, which],
             recv_sem=y_r.at[c, which],
-            device_id={"vocab": to},
+            device_id={"vocab": (up, down)[side if which != 1 else 1 - side]},
             device_id_type=MESH,
         )
 
     def z_copy(c):
-        return pltpu.make_async_remote_copy(
-            src_ref=zst.at[c],
-            dst_ref=r3.at[c],
+        n = 128 if c in ZFIRST else 32
+        return pltpu.make_async_remote_copy(
+            src_ref=zst.at[c, 0:n],
+            dst_ref=r3.at[c, 0:n],
             send_sem=z_s.at[c],
             recv_sem=z_r.at[c],
             device_id={"vocab": across},
             device_id_type=MESH,
         )
 
-    def pair_sum(c, rows, cols):
-        return ownf[c, rows, cols] + sibr[c, rows, cols].astype(F32)
-
-    lo, hi, both = slice(0, HA), slice(HA, HC), slice(0, HC)
-
-    def stage1(c):
-        sib_copy(c).wait_recv()
-        st[c, 128:192, :] = pair_sum(c, slice(128, 192), both).astype(BF)
-        y_copy(c, 0).start()
-        y_copy(c, 1).start()
-        st[c, 64:128, hi] = pair_sum(c, slice(64, 128), hi).astype(BF)
-        y_copy(c, 2).start()
-        st[c, 192:256, lo] = pair_sum(c, slice(192, 256), lo).astype(BF)
-        y_copy(c, 3).start()
-
-    def stage2(c):
-        y_copy(c, 0).wait_recv()
-        st[c, 64:128, lo] = (pair_sum(c, slice(64, 128), lo) + r1[c, 0].astype(F32)).astype(BF)
-        y_copy(c, 4).start()
-        y_copy(c, 1).wait_recv()
-        st[c, 192:256, hi] = (pair_sum(c, slice(192, 256), hi) + r1[c, 1].astype(F32)).astype(BF)
-        y_copy(c, 5).start()
-
-    def stage3(c):
-        for which in (2, 3, 4, 5):
-            y_copy(c, which).wait_recv()
-        away = slice(32, 64)
-        zst[c] = (
-            pair_sum(c, away, both) + r2[c, 0, away].astype(F32) + r2[c, 1, away].astype(F32)
-        ).astype(BF)
-        z_copy(c).start()
-        here = slice(0, 32)
-        ownf[c, here, :] = (
-            pair_sum(c, here, both) + r2[c, 0, here].astype(F32) + r2[c, 1, here].astype(F32)
-        )
-
-    def stage4(c):
-        z_copy(c).wait_recv()
-        total = (ownf[c, 0:32, :] + r3[c].astype(F32)).astype(BF)
-        cols = pl.ds(pl.multiple_of(c * HC, HC), HC)
-        gh_out[0, :, cols] = total[0:16]
-        gh_out[1, :, cols] = total[16:32]
-
-    def when(cond):
-        return pl.when(cond)
-
-    def gh_step(c, carry):
-        cols = pl.ds(pl.multiple_of(c * HC, HC), HC)
-        part = jnp.dot(g[...], wv[:, cols], preferred_element_type=F32)
+    def pair_sum(c, at, n):
+        return ownf[c, at : at + n] + sibr[c, at : at + n].astype(F32)
+
+    def put(c, total):
+        gh_out[0, :, c * HC : (c + 1) * HC] = total[0:16].astype(BF)
+        gh_out[1, :, c * HC : (c + 1) * HC] = total[16:32].astype(BF)
+
+    def y_first(c, stage):
+        forth, back = FORTH[TURN[c]], BACK[TURN[c]]
+        if stage == 1:
+            sib_copy(c).wait_recv()
+            st[c, 128:192] = pair_sum(c, 128, 64).astype(BF)
+            y_copy(c, 0).start()
+            st[c, back : back + 64] = pair_sum(c, back, 64).astype(BF)
+            y_copy(c, 1).start()
+        elif stage == 2:
+            y_copy(c, 0).wait_recv()
+            st[c, forth : forth + 64] = (pair_sum(c, forth, 64) + r1[c].astype(F32)).astype(BF)
+            y_copy(c, 2).start()
+        elif stage == 3:
+            y_copy(c, 1).wait_recv()
+            y_copy(c, 2).wait_recv()
+            total = pair_sum(c, 0, 64) + r2[c, 0].astype(F32) + r2[c, 1].astype(F32)
+            zst[c, 0:32] = total[32:64].astype(BF)
+            z_copy(c).start()
+            ownf[c, 0:32] = total[0:32]
+        else:
+            z_copy(c).wait_recv()
+            put(c, ownf[c, 0:32] + r3[c, 0:32].astype(F32))
+
+    def z_first(c, stage):
+        forth, back = FORTH[TURN[c]], BACK[TURN[c]]
+        if stage == 1:
+            sib_copy(c).wait_recv()
+            for i in range(4):
+                zst[c, 32 * i : 32 * i + 32] = pair_sum(c, 64 * i + 32, 32).astype(BF)
+            z_copy(c).start()
+        elif stage == 2:
+            z_copy(c).wait_recv()
+
+            def total(at):
+                return pair_sum(c, at, 32) + r3[c, at // 2 : at // 2 + 32].astype(F32)
+
+            st[c, 128:160] = total(128).astype(BF)
+            y_copy(c, 0).start()
+            st[c, back : back + 32] = total(back).astype(BF)
+            y_copy(c, 1).start()
+            ownf[c, forth : forth + 32] = total(forth)
+            ownf[c, 0:32] = total(0)
+        elif stage == 3:
+            y_copy(c, 0).wait_recv()
+            st[c, forth : forth + 32] = (
+                ownf[c, forth : forth + 32] + r1[c, 0:32].astype(F32)
+            ).astype(BF)
+            y_copy(c, 2).start()
+        else:
+            y_copy(c, 1).wait_recv()
+            y_copy(c, 2).wait_recv()
+            put(c, ownf[c, 0:32] + r2[c, 0, 0:32].astype(F32) + r2[c, 1, 0:32].astype(F32))
+
+    def at_point(t):
+        for c, stage in PLAN.get(t, ()):
+            if c in ZFIRST:
+                z_first(c, stage)
+            else:
+                y_first(c, stage)
+        if t == 0:
+            for item in far[1]:
+                hx_copy(*item).start()
+        if t == 3:
+            pass_on(1)
+        if t == 6:
+            pass_on(0)
+        if t == 9:
+            pass_on(2)
+
+    for c in range(NH):
+        part = jnp.dot(g[...], wv[:, c * HC : (c + 1) * HC], preferred_element_type=F32)
         sibs[c] = part[256:512].astype(BF)
         sib_copy(c).start()
         ownf[c] = part[0:256]
-
-        @when(c >= 1)
-        def _():
-            stage1(c - 1)
-
-        @when(c >= 4)
-        def _():
-            stage2(c - 4)
-
-        @when(c == 0)
-        def _():
-            for item in far[1]:
-                hx_copy(*item).start()
-
-        @when(c == 2)
-        def _():
-            pass_on(1)
-
-        @when(c == 7)
-        def _():
-            pass_on(0)
-
-        return carry
-
-    lax.fori_loop(0, NH, gh_step, 0)
-    stage1(NH - 1)
-
-    pass_on(2)
-    for which in range(3):
-        fw_copy(which).wait_recv()
+        at_point(c)
 
     token256 = lax.broadcasted_iota(jnp.int32, (L, WC), 0).astype(F32).astype(BF)
 
-    def gw_copy(n, slot, rows):
-        return pltpu.make_async_copy(
-            gwst.at[slot, 0:rows, :],
-            gw_out.at[pl.ds(pl.multiple_of(n * WC, WC), rows), :],
-            gw_sem.at[slot],
-        )
-
-    tail = V - (NW - 1) * WC
-
-    def gw_step(n, carry):
-        slot = n % 2
-        cols = pl.ds(pl.multiple_of(n * WC, WC), WC)
-        for i in range(NK):
-            for s in range(2):
-                spot = pm[i, s : s + 1, cols].astype(BF)
-                val = ds[s, i : i + 1, cols].astype(BF)
-                r = (i * 2 + s) * L
-                gc[r : r + L, :] = jnp.where(token256 == spot, val, jnp.zeros((), BF))
-        out = lax.dot_general(
-            gc[...],
-            hx[...].reshape(NK * 2 * L, DB),
-            (((0,), (0,)), ((), ())),
-            preferred_element_type=F32,
-        )
-
-        @when(n >= 2)
-        def _():
-            gw_copy(n - 2, slot, WC).wait()
-
-        gwst[slot] = out
-
-        @when(n < NW - 1)
-        def _():
-            gw_copy(n, slot, WC).start()
-
-        @when(n == NW - 1)
-        def _():
-            gw_copy(n, slot, tail).start()
-
-        @when(n < 2)
-        def _():
-            stage2(4 + 2 * n)
-            stage2(5 + 2 * n)
-
-        stage3(2 * n)
-        stage3(2 * n + 1)
-
-        @when(n >= 1)
-        def _():
-            stage4(2 * n - 2)
-            stage4(2 * n - 1)
-
-        return carry
-
-    lax.fori_loop(0, NW, gw_step, 0)
-    stage4(NH - 2)
-    stage4(NH - 1)
-
-    gw_copy(NW - 2, (NW - 2) % 2, WC).wait()
-    gw_copy(NW - 1, (NW - 1) % 2, tail).wait()
+    for dz in range(2):
+        base = ((zl + dz) % 2) * 4
+        if dz == 0:
+            fw_copy(0).wait_recv()
+        else:
+            fw_copy(1).wait_recv()
+            fw_copy(2).wait_recv()
+        for n in range(NW):
+            cols = slice(n * WC, (n + 1) * WC)
+            for i in range(4):
+                for s in range(2):
+                    spot = pm[base + i, s : s + 1, cols].astype(BF)
+                    val = ds[s, pl.ds(base + i, 1), cols].astype(BF)
+                    r = (i * 2 + s) * L
+                    gc[r : r + L, :] = jnp.where(token256 == spot, val, jnp.zeros((), BF))
+            out = lax.dot_general(
+                gc[...],
+                hx[pl.ds(base, 4)].reshape(4 * 2 * L, DB),
+                (((0,), (0,)), ((), ())),
+                preferred_element_type=F32,
+            )
+            rows = slice(n * WC, min((n + 1) * WC, V))
+            out = out[0 : rows.stop - rows.start]
+            if dz == 0:
+                gw_out[rows, :] = out
+            else:
+                gw_out[rows, :] += out
+            at_point(NH + dz * NW + n)
+
+    for t in range(NH + 2 * NW, NH + 2 * NW + 4):
+        at_point(t)
+
     for item in near + far[0] + far[1]:
         hx_copy(*item).wait_send()
     for which in range(3):
         fw_copy(which).wait_send()
-
-    def drain(c, carry):
+    for c in range(NH):
         sib_copy(c).wait_send()
-        for which in range(6):
+        for which in range(3):
             y_copy(c, which).wait_send()
         z_copy(c).wait_send()
-        return carry
-
-    lax.fori_loop(0, NH, drain, 0)
-
-
-def finish(gh_in, gw_in, gh_out, gw_out, gh_v, gw_v, in_sem, out_sem):
-    ins = [pltpu.make_async_copy(gh_in, gh_v, in_sem.at[CP])]
-    outs = [pltpu.make_async_copy(gh_v, gh_out, out_sem.at[CP])]
-    for i in range(CP):
-        rows = pl.ds(i * (V // CP), V // CP)
-        ins.append(pltpu.make_async_copy(gw_in.at[rows, :], gw_v.at[rows, :], in_sem.at[i]))
-        outs.append(pltpu.make_async_copy(gw_v.at[rows, :], gw_out.at[rows, :], out_sem.at[i]))
-    for c in ins:
-        c.start()
-    for a, b in zip(ins, outs):
-        a.wait()
-        b.start()
-    for c in outs:
-        c.wait()
 
 
 def local(hidden, weight, bias, positions, lengths, pairs, margins):
@@ -529,16 +498,15 @@
         pltpu.VMEM((2, 2, 2, L // 4, D), BF),
         pltpu.VMEM((NK, 2, 2, 2, L // 4, DB), BF),
         pltpu.VMEM((2 * L, VP), BF),
-        pltpu.VMEM((NK * 2 * L, WC), BF),
-        pltpu.VMEM((2, WC, DB), F32),
+        pltpu.VMEM((NK * L, WC), BF),
         pltpu.VMEM((NH, 256, HC), BF),
         pltpu.VMEM((NH, 256, HC), BF),
         pltpu.VMEM((NH, 256, HC), F32),
         pltpu.VMEM((NH, 256, HC), BF),
-        pltpu.VMEM((NH, 2, 64, HA), BF),
+        pltpu.VMEM((NH, 64, HC), BF),
         pltpu.VMEM((NH, 2, 64, HC), BF),
-        pltpu.VMEM((NH, 32, HC), BF),
-        pltpu.VMEM((NH, 32, HC), BF),
+        pltpu.VMEM((NH, 128, HC), BF),
+        pltpu.VMEM((NH, 128, HC), BF),
         pltpu.VMEM((NK, 4, VP), F32),
         pltpu.VMEM((NK, 2, VP), F32),
         pltpu.VMEM((NJ, NK, 128), F32),
@@ -548,7 +516,6 @@
         dma((NF,)),
         dma,
         dma,
-        dma((2,)),
         dma((7,)),
         dma((7,)),
         dma((7, 2, 2)),
@@ -561,22 +528,22 @@
         dma((NJ,)),
         dma((NH,)),
         dma((NH,)),
-        dma((NH, 6)),
-        dma((NH, 6)),
+        dma((NH, 3)),
+        dma((NH, 3)),
         dma((NH,)),
         dma((NH,)),
     ]
     gh, gw = pl.pallas_call(
         kernel,
         out_shape=(
-            jax.ShapeDtypeStruct((2, 16, D), BF),
-            jax.ShapeDtypeStruct((V, DB), F32),
+            pltpu.VMEM((2, 16, D), BF),
+            pltpu.VMEM((V, DB), F32),
         ),
         in_specs=[hbm, hbm, vmem, vmem, smem, smem, smem],
-        out_specs=(vmem, hbm),
+        out_specs=(vmem, vmem),
         scratch_shapes=scratch,
         compiler_params=pltpu.CompilerParams(
-            collective_id=0, has_side_effects=True, vmem_limit_bytes=62 * 2**20
+            collective_id=0, has_side_effects=True, vmem_limit_bytes=56 * 2**20
         ),
         cost_estimate=pl.CostEstimate(
             flops=6 * 512 * V * D, bytes_accessed=24 * 2**20, transcendentals=0
@@ -591,23 +558,6 @@
         pairs.reshape(2),
         margins,
     )
-    gh, gw = pl.pallas_call(
-        finish,
-        out_shape=(
-            jax.ShapeDtypeStruct((2, 16, D), BF),
-            jax.ShapeDtypeStruct((V, DB), F32),
-        ),
-        in_specs=[hbm, hbm],
-        out_specs=(hbm, hbm),
-        scratch_shapes=[
-            pltpu.VMEM((2, 16, D), BF),
-            pltpu.VMEM((V, DB), F32),
-            dma((CP + 1,)),
-            dma((CP + 1,)),
-        ],
-        compiler_params=pltpu.CompilerParams(vmem_limit_bytes=62 * 2**20),
-        name="finish",
-    )(gh, gw)
     return gh.reshape(2, 1, 16, D), gw
 
 

time: 71.5 us -> 66 us (0.923)
  Pallas kernels: 68.9 us -> 60.9 us
  local copies, waits for them, and re-layouts: 0 us -> 2.68 us
    pallas_call x2 -> x1, Pallas kernels: 68.9 us -> 60.9 us  [local(): pl.pallas_call(kernel, out_shape=(pltpu.VMEM((2, 16, D), BF), pltpu.VMEM(...]
    unnamed x0 -> x2, local copies, waits for them, and re-layouts: none -> 2.68 us
where the time goes in v3:
time: 66 us; the launch traced here: 64.9 us
  Pallas kernels  60.9 us (92%)
  local copies, waits for them, and re-layouts  2.68 us (4%)
  between operations  1.29 us (2%)
    pallas_call x1, Pallas kernels, local(): pl.pallas_call(kernel, out_shape=(pltpu.VMEM((2, 16, D), BF), pltpu.VMEM(...  60.9 us
    unnamed x2, local copies, waits for them, and re-layouts  2.68 us

profile of v3, /device:TPU:2, one launch (start us, length us, event | category | flops | bytes accessed | tf_op | source)
XLA Modules:
  0.0 64.9 jit_solution(10096079041283189099)
XLA Ops:
  1.3 60.9 %splade_backward.1 = (bf16[2,16,4096]{2,1,0:T(8,128)(2,1)S(1)}, f32[2000,512]{1,0:T(8,128)S(1)}) custom-call(bf16[2,2,2,64,4096]{4,3,2,1,0:T(8,128)(2,1)} %bitcast.8, bf16[2000,4096]{1,0:T(8,128)(2,1)} %w_hbm.1, f32[1,2000]{1,0:T(1,128)} %bitcast.9, s32[2,1,2000]{2,1,0:T(1,128)} %pos_in.1, s32[2]{0:T(128)} %bitcast.10, s32[2]{0:T(128)} %bitcast.11, ...), custom_call_target="tpu_custom_call" | custom-call | flops 25165824000 | bytes 25165824 | tf_op jit(solution)/shard_map/splade_backward/pallas_call | solution.py:536
  62.2 0.7 %copy.12 = bf16[2,1,16,4096]{3,2,1,0:T(8,128)(2,1)} copy(bf16[2,1,16,4096]{3,2,1,0:T(8,128)(2,1)S(1)} %bitcast.7) | data formatting | bytes 524288
  62.9 2.0 %copy.13 = f32[2000,512]{1,0:T(8,128)} copy(f32[2000,512]{1,0:T(8,128)S(1)} %get-tuple-element.9) | data formatting | bytes 8192000

commit v4 on v3

--- a/solution.py
+++ b/solution.py
@@ -26,8 +26,8 @@
 NH = D // HC
 WC = 512
 NW = VP // WC
-ZFIRST = (0, 3, 7)
-TURN = (0, 1, 0, 1, 1, 0, 1, 0)
+ZFIRST = (0, 4, 7)
+TURN = (0, 1, 0, 1, 1, 1, 0, 0)
 FORTH, BACK = (64, 192), (192, 64)
 PLAN = {
     2: ((0, 1),),
@@ -36,13 +36,13 @@
     5: ((3, 1),),
     6: ((1, 2), (4, 1), (5, 1)),
     7: ((0, 2), (2, 2)),
-    8: ((1, 3), (6, 1), (7, 1)),
-    9: ((3, 2), (4, 2), (5, 2)),
-    10: ((0, 3),),
-    11: ((1, 4), (2, 3), (6, 2)),
-    12: ((3, 3), (7, 2)),
-    13: ((0, 4), (4, 3), (5, 3)),
-    14: ((2, 4), (3, 4), (6, 3), (7, 3)),
+    8: ((3, 2), (1, 3), (6, 1), (7, 1)),
+    9: ((0, 3), (5, 2)),
+    10: ((2, 3), (4, 2), (3, 3), (1, 4)),
+    11: ((0, 4), (6, 2)),
+    12: ((5, 3), (7, 2)),
+    13: ((2, 4), (3, 4), (4, 3)),
+    14: ((6, 3), (7, 3)),
     15: ((4, 4), (5, 4), (7, 4), (6, 4)),
 }
 
@@ -116,10 +116,32 @@
     across = vid(1, 0, 0)
     dp_steps = [(dz, dx) for dz in range(2) for dx in range(4) if (dz, dx) != (0, 0)]
 
+    halves = (slice(0, D // 2), slice(D // 2, D))
+    h_copies = [
+        pltpu.make_async_copy(h_hbm.at[..., cols], hv.at[..., cols], h_sem.at[i])
+        for i, cols in enumerate(halves)
+    ]
+    w0_copies = [
+        pltpu.make_async_copy(
+            w_hbm.at[0 : FWD[0][1], cols], wv.at[0 : FWD[0][1], cols], w_sem.at[(0, NF)[i]]
+        )
+        for i, cols in enumerate(halves)
+    ]
+    w_copies = [None]
+    for n, (at, size) in enumerate(FWD):
+        if n > 0:
+            rows = min(size, V - at)
+            c = pltpu.make_async_copy(
+                w_hbm.at[pl.ds(at, rows), :], wv.at[pl.ds(at, rows), :], w_sem.at[n]
+            )
+            w_copies.append(c)
+    h_copies[0].start()
+    w0_copies[0].start()
+
     barrier = pltpu.get_barrier_semaphore()
     for dz, dx in dp_steps:
         pl.semaphore_signal(barrier, inc=1, device_id={"dp": kid(dz, dx)}, device_id_type=MESH)
-    for dx in range(4):
+    for dx in range(1, 4):
         pl.semaphore_signal(
             barrier,
             inc=1,
@@ -127,19 +149,17 @@
             device_id_type=MESH,
         )
     for i in range(1, NJ):
-        pl.semaphore_signal(barrier, inc=1, device_id={"vocab": (j + i) % NJ}, device_id_type=MESH)
-
-    h_copy = pltpu.make_async_copy(h_hbm, hv, h_sem)
-    h_copy.start()
-    w_copies = []
-    for n, (at, size) in enumerate(FWD):
-        rows = min(size, V - at)
-        c = pltpu.make_async_copy(
-            w_hbm.at[pl.ds(at, rows), :], wv.at[pl.ds(at, rows), :], w_sem.at[n]
-        )
-        w_copies.append(c)
-    w_copies[0].start()
-    w_copies[1].start()
+        zr, yr, cr = i // 8, (i // 2) % 4, i % 2
+        pl.semaphore_signal(
+            barrier,
+            inc=1,
+            device_id={"dp": kid(zr, 0), "vocab": vid(zr, yr, cr)},
+            device_id_type=MESH,
+        )
+    pl.semaphore_signal(barrier, inc=1, device_id={"vocab": across}, device_id_type=MESH)
+
+    h_copies[1].start()
+    w0_copies[1].start()
     own_copy = pltpu.make_async_copy(
         hv.at[core, :, :, :, pl.ds(pl.multiple_of(k * DB, DB), DB)],
         hx.at[k, core],
@@ -216,23 +236,36 @@
             hx_copy(*item).wait_recv()
         fw_copy(which).start()
 
-    h_copy.wait()
-    pl.semaphore_wait(barrier, len(dp_steps) + 4 + NJ - 1)
+    def logits(rows, cols):
+        return lax.dot_general(
+            hv[..., cols].reshape(2 * L, cols.stop - cols.start),
+            wv[rows, cols],
+            (((1,), (1,)), ((), ())),
+            preferred_element_type=F32,
+        )
+
+    pl.semaphore_wait(barrier, len(dp_steps) + 3 + NJ)
     for i in range(7):
         to_dp(pm, pm_s, pm_r, i).start()
-    for item in far[0]:
-        hx_copy(*item).start()
-    own_copy.start()
     for n, (at, size) in enumerate(FWD):
-        w_copies[n].wait()
-        if n + 2 < NF:
-            w_copies[n + 2].start()
-        lg = lax.dot_general(
-            hv[...].reshape(2 * L, D),
-            wv[at : at + size, :],
-            (((1,), (1,)), ((), ())),
-            preferred_element_type=F32,
-        )
+        rows = slice(at, at + size)
+        if n == 0:
+            h_copies[0].wait()
+            w0_copies[0].wait()
+            w_copies[1].start()
+            lg = logits(rows, halves[0])
+            h_copies[1].wait()
+            w0_copies[1].wait()
+            for item in far[0]:
+                hx_copy(*item).start()
+            own_copy.start()
+            w_copies[2].start()
+            lg += logits(rows, halves[1])
+        else:
+            w_copies[n].wait()
+            if 2 < n + 2 < NF:
+                w_copies[n + 2].start()
+            lg = logits(rows, slice(0, D))
         token = lax.broadcasted_iota(jnp.int32, (L, size), 0).astype(F32)
         width = min(size, V - at)
         for s in range(2):
@@ -249,21 +282,18 @@
     for i in range(7):
         to_dp(sel, sel_s, sel_r, i).start()
     for i in range(7):
-        to_dp(pm, pm_s, pm_r, i).wait()
+        to_dp(pm, pm_s, pm_r, i).wait_recv()
+    first = jnp.concatenate([pm[i, 2:3, 0:128] for i in range(NK)], axis=0)
+    second = jnp.concatenate([pm[i, 2:3, 128:256] for i in range(NK)], axis=0)
+    margin = jnp.concatenate([pm[i, 2:3, 256:384] for i in range(NK)], axis=0)
+
     for i in range(7):
-        to_dp(sel, sel_s, sel_r, i).wait()
-    for item in near:
-        hx_copy(*item).start()
-
+        to_dp(sel, sel_s, sel_r, i).wait_recv()
     for i in range(NK):
         qs[i : i + 1, :] = sel[i, 0:1, :]
         ps[i : i + 1, :] = sel[i, 1:2, :]
     q = jnp.log1p(qs[...])
     p = jnp.log1p(ps[...])
-    first = jnp.concatenate([pm[i, 2:3, 0:128] for i in range(NK)], axis=0)
-    second = jnp.concatenate([pm[i, 2:3, 128:256] for i in range(NK)], axis=0)
-    margin = jnp.concatenate([pm[i, 2:3, 256:384] for i in range(NK)], axis=0)
-
     def hit(a, b):
         return jnp.where(a == b, 1.0, 0.0)
 
@@ -274,17 +304,20 @@
     dl[j] = jnp.broadcast_to(jnp.sum(q * diff, axis=1, keepdims=True), (NK, 128))
 
     def dl_copy(i):
+        zr, yr, cr = i // 8, (i // 2) % 4, i % 2
         return pltpu.make_async_remote_copy(
             src_ref=dl.at[j],
             dst_ref=dl.at[j],
             send_sem=dl_s.at[i],
             recv_sem=dl_r.at[i],
-            device_id={"vocab": (j + i) % NJ},
+            device_id={"dp": kid(zr, 0), "vocab": vid(zr, yr, cr)},
             device_id_type=MESH,
         )
 
     for i in range(1, NJ):
         dl_copy(i).start()
+    for item in near:
+        hx_copy(*item).start()
 
     reg = objective_factor * regularizer_coefficient * 2.0 / NK / NK
     mean_q = reg * jnp.sum(q, axis=0, keepdims=True)
@@ -293,7 +326,7 @@
     inv_p = jnp.where(ps[...] > 0.0, 1.0 / (1.0 + ps[...]), 0.0)
 
     for i in range(1, NJ):
-        dl_copy(i).wait()
+        dl_copy(i).wait_recv()
     delta = dl[0]
     for i in range(1, NJ):
         delta += dl[i]
@@ -477,6 +510,11 @@
     for t in range(NH + 2 * NW, NH + 2 * NW + 4):
         at_point(t)
 
+    for i in range(7):
+        to_dp(pm, pm_s, pm_r, i).wait_send()
+        to_dp(sel, sel_s, sel_r, i).wait_send()
+    for i in range(1, NJ):
+        dl_copy(i).wait_send()
     for item in near + far[0] + far[1]:
         hx_copy(*item).wait_send()
     for which in range(3):
@@ -513,8 +551,8 @@
         pltpu.VMEM((NK, VP), F32),
         pltpu.VMEM((NK, VP), F32),
         pltpu.VMEM((2, NK, VP), F32),
-        dma((NF,)),
-        dma,
+        dma((NF + 1,)),
+        dma((2,)),
         dma,
         dma((7,)),
         dma((7,)),

time: 66 us -> 64.5 us (0.977); the launches traced: 64.9 us -> 64.3 us
  no operation moved by 1% of the time
where the time goes in v4:
time: 64.5 us; the launch traced here: 64.3 us
  Pallas kernels  60.4 us (94%)
  local copies, waits for them, and re-layouts  2.68 us (4%)
  between operations  1.29 us (2%)
    pallas_call x1, Pallas kernels, local(): pl.pallas_call(kernel, out_shape=(pltpu.VMEM((2, 16, D), BF), pltpu.VMEM(...  60.4 us
    unnamed x2, local copies, waits for them, and re-layouts  2.68 us

profile of v4, /device:TPU:2, one launch (start us, length us, event | category | flops | bytes accessed | tf_op | source)
XLA Modules:
  0.0 64.3 jit_solution(17383115689093794699)
XLA Ops:
  1.3 60.4 %splade_backward.1 = (bf16[2,16,4096]{2,1,0:T(8,128)(2,1)S(1)}, f32[2000,512]{1,0:T(8,128)S(1)}) custom-call(bf16[2,2,2,64,4096]{4,3,2,1,0:T(8,128)(2,1)} %bitcast.8, bf16[2000,4096]{1,0:T(8,128)(2,1)} %w_hbm.1, f32[1,2000]{1,0:T(1,128)} %bitcast.9, s32[2,1,2000]{2,1,0:T(1,128)} %pos_in.1, s32[2]{0:T(128)} %bitcast.10, s32[2]{0:T(128)} %bitcast.11, ...), custom_call_target="tpu_custom_call" | custom-call | flops 25165824000 | bytes 25165824 | tf_op jit(solution)/shard_map/splade_backward/pallas_call | solution.py:574
  61.6 0.7 %copy.12 = bf16[2,1,16,4096]{3,2,1,0:T(8,128)(2,1)} copy(bf16[2,1,16,4096]{3,2,1,0:T(8,128)(2,1)S(1)} %bitcast.7) | data formatting | bytes 524288
  62.3 2.0 %copy.13 = f32[2000,512]{1,0:T(8,128)} copy(f32[2000,512]{1,0:T(8,128)S(1)} %get-tuple-element.9) | data formatting | bytes 8192000

commit v5 on v4

--- a/solution.py
+++ b/solution.py
@@ -176,13 +176,23 @@
     pm[k, 2:3, 384:VP] = jnp.zeros((1, VP - 384), F32)
     pm[k, 3:4, :] = jnp.zeros((1, VP), F32)
 
+    def all_of(ref, ssem, rsem):
+        return pltpu.make_async_remote_copy(
+            src_ref=ref,
+            dst_ref=ref,
+            send_sem=ssem,
+            recv_sem=rsem,
+            device_id={"vocab": sibling},
+            device_id_type=MESH,
+        )
+
     def to_dp(ref, ssem, rsem, i):
         dz, dx = dp_steps[i]
         return pltpu.make_async_remote_copy(
             src_ref=ref.at[k],
             dst_ref=ref.at[k],
-            send_sem=ssem.at[i],
-            recv_sem=rsem.at[i],
+            send_sem=ssem,
+            recv_sem=rsem,
             device_id={"dp": kid(dz, dx)},
             device_id_type=MESH,
         )
@@ -206,7 +216,7 @@
         return pltpu.make_async_remote_copy(
             src_ref=src,
             dst_ref=dst,
-            send_sem=hx_s.at[sems],
+            send_sem=hx_s.at[0 if part is None else 1 + sub],
             recv_sem=hx_r.at[sems],
             device_id=to,
             device_id_type=MESH,
@@ -281,14 +291,12 @@
 
     for i in range(7):
         to_dp(sel, sel_s, sel_r, i).start()
-    for i in range(7):
-        to_dp(pm, pm_s, pm_r, i).wait_recv()
+    all_of(pm.at[0:7], pm_s, pm_r).wait_recv()
     first = jnp.concatenate([pm[i, 2:3, 0:128] for i in range(NK)], axis=0)
     second = jnp.concatenate([pm[i, 2:3, 128:256] for i in range(NK)], axis=0)
     margin = jnp.concatenate([pm[i, 2:3, 256:384] for i in range(NK)], axis=0)
 
-    for i in range(7):
-        to_dp(sel, sel_s, sel_r, i).wait_recv()
+    all_of(sel.at[0:7], sel_s, sel_r).wait_recv()
     for i in range(NK):
         qs[i : i + 1, :] = sel[i, 0:1, :]
         ps[i : i + 1, :] = sel[i, 1:2, :]
@@ -308,8 +316,8 @@
         return pltpu.make_async_remote_copy(
             src_ref=dl.at[j],
             dst_ref=dl.at[j],
-            send_sem=dl_s.at[i],
-            recv_sem=dl_r.at[i],
+            send_sem=dl_s,
+            recv_sem=dl_r,
             device_id={"dp": kid(zr, 0), "vocab": vid(zr, yr, cr)},
             device_id_type=MESH,
         )
@@ -325,8 +333,7 @@
     inv_q = jnp.where(qs[...] > 0.0, 1.0 / (1.0 + qs[...]), 0.0)
     inv_p = jnp.where(ps[...] > 0.0, 1.0 / (1.0 + ps[...]), 0.0)
 
-    for i in range(1, NJ):
-        dl_copy(i).wait_recv()
+    all_of(dl.at[1:NJ], dl_s, dl_r).wait_recv()
     delta = dl[0]
     for i in range(1, NJ):
         delta += dl[i]
@@ -359,7 +366,7 @@
         return pltpu.make_async_remote_copy(
             src_ref=sibs.at[c],
             dst_ref=sibr.at[c],
-            send_sem=sib_s.at[c],
+            send_sem=sib_s,
             recv_sem=sib_r.at[c],
             device_id={"vocab": sibling},
             device_id_type=MESH,
@@ -376,7 +383,7 @@
         return pltpu.make_async_remote_copy(
             src_ref=src,
             dst_ref=dst,
-            send_sem=y_s.at[c, which],
+            send_sem=y_s.at[c],
             recv_sem=y_r.at[c, which],
             device_id={"vocab": (up, down)[side if which != 1 else 1 - side]},
             device_id_type=MESH,
@@ -510,20 +517,18 @@
     for t in range(NH + 2 * NW, NH + 2 * NW + 4):
         at_point(t)
 
-    for i in range(7):
-        to_dp(pm, pm_s, pm_r, i).wait_send()
-        to_dp(sel, sel_s, sel_r, i).wait_send()
-    for i in range(1, NJ):
-        dl_copy(i).wait_send()
-    for item in near + far[0] + far[1]:
-        hx_copy(*item).wait_send()
+    all_of(pm.at[0:7], pm_s, pm_r).wait_send()
+    all_of(sel.at[0:7], sel_s, sel_r).wait_send()
+    all_of(dl.at[1:NJ], dl_s, dl_r).wait_send()
+    all_of(hx.at[0:3, 0], hx_s.at[0], hx_r.at[0, 0, 0]).wait_send()
+    for sub in range(2):
+        all_of(hx.at[0:2, 0], hx_s.at[1 + sub], hx_r.at[0, 0, 0]).wait_send()
     for which in range(3):
         fw_copy(which).wait_send()
     for c in range(NH):
-        sib_copy(c).wait_send()
-        for which in range(3):
-            y_copy(c, which).wait_send()
+        all_of(st.at[c, 0 : 3 * height(c)], y_s.at[c], y_r.at[c, 0]).wait_send()
         z_copy(c).wait_send()
+    all_of(sibs, sib_s, sib_r.at[0]).wait_send()
 
 
 def local(hidden, weight, bias, positions, lengths, pairs, margins):
@@ -554,19 +559,19 @@
         dma((NF + 1,)),
         dma((2,)),
         dma,
-        dma((7,)),
-        dma((7,)),
-        dma((7, 2, 2)),
+        dma,
+        dma,
+        dma((3,)),
         dma((7, 2, 2)),
         dma((3,)),
         dma((3,)),
-        dma((7,)),
-        dma((7,)),
-        dma((NJ,)),
-        dma((NJ,)),
+        dma,
+        dma,
+        dma,
+        dma,
+        dma,
         dma((NH,)),
         dma((NH,)),
-        dma((NH, 3)),
         dma((NH, 3)),
         dma((NH,)),
         dma((NH,)),

time: 64.5 us -> 63.5 us (0.984)
  Pallas kernels: 60.4 us -> 59.3 us
    pallas_call x1, Pallas kernels: 60.4 us -> 59.3 us  [local(): pl.pallas_call(kernel, out_shape=(pltpu.VMEM((2, 16, D), BF), pltpu.VMEM(...]
where the time goes in v5:
time: 63.5 us; the launch traced here: 63.3 us
  Pallas kernels  59.3 us (93%)
  local copies, waits for them, and re-layouts  2.68 us (4%)
  between operations  1.29 us (2%)
    pallas_call x1, Pallas kernels, local(): pl.pallas_call(kernel, out_shape=(pltpu.VMEM((2, 16, D), BF), pltpu.VMEM(...  59.3 us
    unnamed x2, local copies, waits for them, and re-layouts  2.68 us

profile of v5, /device:TPU:2, one launch (start us, length us, event | category | flops | bytes accessed | tf_op | source)
XLA Modules:
  0.0 63.3 jit_solution(16626204808850554039)
XLA Ops:
  1.3 59.3 %splade_backward.1 = (bf16[2,16,4096]{2,1,0:T(8,128)(2,1)S(1)}, f32[2000,512]{1,0:T(8,128)S(1)}) custom-call(bf16[2,2,2,64,4096]{4,3,2,1,0:T(8,128)(2,1)} %bitcast.8, bf16[2000,4096]{1,0:T(8,128)(2,1)} %w_hbm.1, f32[1,2000]{1,0:T(1,128)} %bitcast.9, s32[2,1,2000]{2,1,0:T(1,128)} %pos_in.1, s32[2]{0:T(128)} %bitcast.10, s32[2]{0:T(128)} %bitcast.11, ...), custom_call_target="tpu_custom_call" | custom-call | flops 25165824000 | bytes 25165824 | tf_op jit(solution)/shard_map/splade_backward/pallas_call | solution.py:579
  60.6 0.7 %copy.12 = bf16[2,1,16,4096]{3,2,1,0:T(8,128)(2,1)} copy(bf16[2,1,16,4096]{3,2,1,0:T(8,128)(2,1)S(1)} %bitcast.7) | data formatting | bytes 524288
  61.3 2.0 %copy.13 = f32[2000,512]{1,0:T(8,128)} copy(f32[2000,512]{1,0:T(8,128)S(1)} %get-tuple-element.9) | data formatting | bytes 8192000

commit v6 on v5

--- a/solution.py
+++ b/solution.py
@@ -208,16 +208,16 @@
         other = kid(dz, dx)
         cols = pl.ds(pl.multiple_of(other * DB, DB), DB)
         if part is None:
-            src, dst, sems = hv.at[core, :, :, :, cols], hx.at[k, core], (i, 0, 0)
+            src, dst = hv.at[core, :, :, :, cols], hx.at[k, core]
             to = {"dp": other}
         else:
             src, dst = hv.at[core, part, sub, :, cols], hx.at[k, core, part, sub]
-            sems, to = (i, part, sub), {"dp": other, "vocab": vid(part, 0, 0)}
+            to = {"dp": other, "vocab": vid(part, 0, 0)}
         return pltpu.make_async_remote_copy(
             src_ref=src,
             dst_ref=dst,
             send_sem=hx_s.at[0 if part is None else 1 + sub],
-            recv_sem=hx_r.at[sems],
+            recv_sem=hx_r.at[0 if part is None else 1 + sub],
             device_id=to,
             device_id_type=MESH,
         )
@@ -239,11 +239,7 @@
     def pass_on(which):
         if which == 0:
             own_copy.wait()
-            batch = near
-        else:
-            batch = far[which - 1]
-        for item in batch:
-            hx_copy(*item).wait_recv()
+        all_of(hx.at[0 : 3 if which == 0 else 2, 0], hx_s.at[which], hx_r.at[which]).wait_recv()
         fw_copy(which).start()
 
     def logits(rows, cols):
@@ -384,7 +380,7 @@
             src_ref=src,
             dst_ref=dst,
             send_sem=y_s.at[c],
-            recv_sem=y_r.at[c, which],
+            recv_sem=y_r.at[c, min(which, 1)],
             device_id={"vocab": (up, down)[side if which != 1 else 1 - side]},
             device_id_type=MESH,
         )
@@ -420,8 +416,7 @@
             st[c, forth : forth + 64] = (pair_sum(c, forth, 64) + r1[c].astype(F32)).astype(BF)
             y_copy(c, 2).start()
         elif stage == 3:
-            y_copy(c, 1).wait_recv()
-            y_copy(c, 2).wait_recv()
+            all_of(r2.at[c, :, 0 : height(c)], y_s.at[c], y_r.at[c, 1]).wait_recv()
             total = pair_sum(c, 0, 64) + r2[c, 0].astype(F32) + r2[c, 1].astype(F32)
             zst[c, 0:32] = total[32:64].astype(BF)
             z_copy(c).start()
@@ -456,8 +451,7 @@
             ).astype(BF)
             y_copy(c, 2).start()
         else:
-            y_copy(c, 1).wait_recv()
-            y_copy(c, 2).wait_recv()
+            all_of(r2.at[c, :, 0 : height(c)], y_s.at[c], y_r.at[c, 1]).wait_recv()
             put(c, ownf[c, 0:32] + r2[c, 0, 0:32].astype(F32) + r2[c, 1, 0:32].astype(F32))
 
     def at_point(t):
@@ -520,9 +514,9 @@
     all_of(pm.at[0:7], pm_s, pm_r).wait_send()
     all_of(sel.at[0:7], sel_s, sel_r).wait_send()
     all_of(dl.at[1:NJ], dl_s, dl_r).wait_send()
-    all_of(hx.at[0:3, 0], hx_s.at[0], hx_r.at[0, 0, 0]).wait_send()
+    all_of(hx.at[0:3, 0], hx_s.at[0], hx_r.at[0]).wait_send()
     for sub in range(2):
-        all_of(hx.at[0:2, 0], hx_s.at[1 + sub], hx_r.at[0, 0, 0]).wait_send()
+        all_of(hx.at[0:2, 0], hx_s.at[1 + sub], hx_r.at[0]).wait_send()
     for which in range(3):
         fw_copy(which).wait_send()
     for c in range(NH):
@@ -562,9 +556,9 @@
         dma,
         dma,
         dma((3,)),
-        dma((7, 2, 2)),
         dma((3,)),
         dma((3,)),
+        dma((3,)),
         dma,
         dma,
         dma,
@@ -572,7 +566,7 @@
         dma,
         dma((NH,)),
         dma((NH,)),
-        dma((NH, 3)),
+        dma((NH, 2)),
         dma((NH,)),
         dma((NH,)),
     ]

time: 63.5 us -> 63.2 us (level)
  no operation moved by 1% of the time
where the time goes in v6:
time: 63.2 us; the launch traced here: 63 us
  Pallas kernels  59.1 us (94%)
  local copies, waits for them, and re-layouts  2.68 us (4%)
  between operations  1.29 us (2%)
    pallas_call x1, Pallas kernels, local(): pl.pallas_call(kernel, out_shape=(pltpu.VMEM((2, 16, D), BF), pltpu.VMEM(...  59.1 us
    unnamed x2, local copies, waits for them, and re-layouts  2.68 us

profile of v6, /device:TPU:2, one launch (start us, length us, event | category | flops | bytes accessed | tf_op | source)
XLA Modules:
  0.0 63.0 jit_solution(14768309244704142273)
XLA Ops:
  1.3 59.1 %splade_backward.1 = (bf16[2,16,4096]{2,1,0:T(8,128)(2,1)S(1)}, f32[2000,512]{1,0:T(8,128)S(1)}) custom-call(bf16[2,2,2,64,4096]{4,3,2,1,0:T(8,128)(2,1)} %bitcast.8, bf16[2000,4096]{1,0:T(8,128)(2,1)} %w_hbm.1, f32[1,2000]{1,0:T(1,128)} %bitcast.9, s32[2,1,2000]{2,1,0:T(1,128)} %pos_in.1, s32[2]{0:T(128)} %bitcast.10, s32[2]{0:T(128)} %bitcast.11, ...), custom_call_target="tpu_custom_call" | custom-call | flops 25165824000 | bytes 25165824 | tf_op jit(solution)/shard_map/splade_backward/pallas_call | solution.py:573
  60.4 0.7 %copy.12 = bf16[2,1,16,4096]{3,2,1,0:T(8,128)(2,1)} copy(bf16[2,1,16,4096]{3,2,1,0:T(8,128)(2,1)S(1)} %bitcast.7) | data formatting | bytes 524288
  61.1 2.0 %copy.13 = f32[2000,512]{1,0:T(8,128)} copy(f32[2000,512]{1,0:T(8,128)S(1)} %get-tuple-element.9) | data formatting | bytes 8192000
